TPU v7x, 512 devices: a whole 4x8x8 slice. The times are simulated.
512 devices in a mesh: row: 32 (over y, x), col: 16 (over z, core).
Axes of the slice: x: 4, y: 8, z: 8, core: 2. Of those that a mesh axis runs over, the one named last changes fastest.
Arguments:
- matrix: float32 [12288, 12288], P('row', 'col'), may hold values from 0 to 2, as said below
Outputs:
- factored: float32 [12288, 12288], P('row', 'col')
Inputs may be any that keep to these rules, and one draw needn't show every extreme that they name: `matrix`: symmetric positive definite: a Matern kernel of smoothness 3/2 over points, plus a positive noise term on the diagonal.
All inputs are finite; a program needn't handle non-finite values.
Results may differ from a plain program's by a relative error of at most 0.0003.
Values sent between devices are 32-bit elements; how exact they have to be, the bound alone decides.
No kernel may reach another device: no remote copies, remote signals or barrier semaphores. Data moves between devices by JAX's collectives and lax.ppermute only.
A program may use at most 64 MiB of HBM per device.

v0:
```python
import jax
import jax.numpy as jnp
from jax import lax
from jax.sharding import PartitionSpec as P

NB = 512
PANELS = 2


def spread(block, axis, holder):
    block = jnp.where(lax.axis_index(axis) == holder, block, jnp.zeros_like(block))
    return lax.psum(block, axis)


def shards(matrix):
    rows_local, cols_local = matrix.shape
    grid_rows = lax.axis_size("row")
    grid_cols = lax.axis_size("col")
    block_width = NB // grid_cols
    row_id = lax.axis_index("row")
    col_id = lax.axis_index("col")
    local_rows = jnp.arange(rows_local, dtype=jnp.int32)
    local_cols = jnp.arange(cols_local, dtype=jnp.int32)
    logical_rows = (
        local_rows // block_width * grid_rows + row_id
    ) * block_width + local_rows % block_width
    logical_cols = (
        local_cols // block_width * grid_cols + col_id
    ) * block_width + local_cols % block_width
    current = matrix
    for panel_index in range(PANELS):
        start_col = panel_index * NB
        end_col = start_col + NB
        thin_slice = current[:, panel_index * block_width : (panel_index + 1) * block_width]
        columns = lax.all_gather(thin_slice, "col", axis=1, tiled=True)
        stacked = lax.all_gather(columns[0:block_width], "row", axis=0, tiled=True)
        factor = jnp.linalg.cholesky(stacked[start_col:end_col])
        solved = jax.scipy.linalg.solve_triangular(factor, columns.T, lower=True).T
        row_panel = jnp.where((logical_rows >= start_col)[:, None], solved, 0.0)
        from_low = spread(row_panel, "row", col_id)
        from_high = spread(row_panel, "row", col_id + grid_cols)
        paired = jnp.stack(
            [from_low.reshape(-1, block_width, NB), from_high.reshape(-1, block_width, NB)], axis=1
        )
        col_panel = paired.reshape(cols_local, NB)
        row_trail = jnp.where((logical_rows >= end_col)[:, None], row_panel, 0.0)
        col_trail = jnp.where((logical_cols >= end_col)[:, None], col_panel, 0.0)
        current = current - jnp.dot(row_trail, col_trail.T, precision=lax.Precision.HIGHEST)
        own_piece = lax.dynamic_slice_in_dim(row_panel, col_id * block_width, block_width, 1)
        current = jnp.concatenate(
            [
                current[:, : panel_index * block_width],
                own_piece,
                current[:, (panel_index + 1) * block_width :],
            ],
            axis=1,
        )
    return current


def solution(mesh):
    placed = (P("row", "col"),)
    return jax.shard_map(
        shards, mesh=mesh, in_specs=placed, out_specs=P("row", "col"), check_vma=False
    )
```

profile of v0, /device:TPU:1, one launch (start us, length us, event | category | flops | bytes accessed | tf_op | source)
XLA Modules:
  0.0 848.9 jit_solution(3531589180254002348)
XLA Ops:
  6.5 0.9 slice.108
  7.6 26.7 %all_gather.12 = f32[384,512]{0,1:T(8,128)S(1)} all-gather(f32[384,32]{0,1:T(8,128)S(1)} %copy.55), channel_id=1, replica_groups=mesh['row'=32,'col'=16] {'col'}, dimensions={1}, use_global_device_ids=true | all-gather | bytes 835584 | tf_op jit(solution)/shard_map/all_gather | solution.py:35
  34.2 0.7 copy.40
  35.1 76.2 %all-gather.3.cloned.1.call-done = f32[1024,512]{1,0:T(8,128)} async-done(((f32[32,512]{1,0:T(8,128)}), f32[1024,512]{1,0:T(8,128)}) %all-gather.3.cloned.1.call-update) | async-done | bytes 2097168 | tf_op jit(solution)/shard_map/all_gather | solution.py:36
  111.3 1.2 slice-done
  112.8 1.4 fusion.1
  114.3 11.7 %cholesky.286 = f32[128,128]{1,0:T(8,128)S(1)} custom-call(f32[128,128]{1,0:T(8,128)S(1)} %cholesky.426), custom_call_target="Cholesky" | custom-call | tf_op jit(solution)/shard_map/jit(cholesky)/cholesky | solution.py:37
  126.0 9.8 %custom-call.27 = f32[1,128,128]{1,2,0:T(8,128)S(1)} custom-call(f32[1,128,128]{2,1,0:T(8,128)S(1)} %get-tuple-element.70), custom_call_target="InvertDiagBlocksLowerTriangular" | custom-call | tf_op jit(solution)/shard_map/jit(cholesky)/cholesky | solution.py:37
  136.7 11.7 %cholesky.305 = f32[128,128]{1,0:T(8,128)S(1)} custom-call(f32[128,128]{1,0:T(8,128)S(1)} %cholesky.430), custom_call_target="Cholesky" | custom-call | tf_op jit(solution)/shard_map/jit(cholesky)/cholesky | solution.py:37
  148.4 10.0 %custom-call.28 = f32[1,128,128]{1,2,0:T(8,128)S(1)} custom-call(f32[1,128,128]{2,1,0:T(8,128)S(1)} %get-tuple-element.67), custom_call_target="InvertDiagBlocksLowerTriangular" | custom-call | tf_op jit(solution)/shard_map/jit(cholesky)/cholesky | solution.py:37
  159.1 11.7 %cholesky.326 = f32[128,128]{1,0:T(8,128)S(1)} custom-call(f32[128,128]{1,0:T(8,128)S(1)} %cholesky.435), custom_call_target="Cholesky" | custom-call | tf_op jit(solution)/shard_map/jit(cholesky)/cholesky | solution.py:37
  171.5 9.8 %custom-call.29 = f32[1,128,128]{1,2,0:T(8,128)S(1)} custom-call(f32[1,128,128]{2,1,0:T(8,128)S(1)} %get-tuple-element.64), custom_call_target="InvertDiagBlocksLowerTriangular" | custom-call | tf_op jit(solution)/shard_map/jit(cholesky)/cholesky | solution.py:37
  182.0 11.7 %cholesky.343 = f32[128,128]{1,0:T(8,128)S(1)} custom-call(f32[128,128]{1,0:T(8,128)S(1)} %convolution_subtract_fusion.13), custom_call_target="Cholesky" | custom-call | tf_op jit(solution)/shard_map/jit(cholesky)/cholesky | solution.py:37
  198.1 8.5 while.4
  198.8 1.4 bitcast_dynamic-update-slice_fusion.4
  200.9 1.4 bitcast_dynamic-update-slice_fusion.4
  203.0 1.4 bitcast_dynamic-update-slice_fusion.4
  205.2 1.4 bitcast_dynamic-update-slice_fusion.4
  206.6 39.3 %custom-call.30 = f32[4,128,128]{1,2,0:T(8,128)S(1)} custom-call(f32[4,128,128]{2,1,0:T(8,128)S(1)} %get-tuple-element.21), custom_call_target="InvertDiagBlocksLowerTriangular" | custom-call | tf_op jit(solution)/shard_map/jit(_solve_triangular)/triangular_solve | solution.py:38
  248.8 1.2 copy.43
  250.1 1.1 copy.44
  251.3 159.8 %all-reduce.8.cloned.1.call-done = (f32[12,1,32,512]{3,2,0,1:T(8,128)}, f32[12,1,32,512]{3,2,0,1:T(8,128)}) async-done(((f32[12,1,32,512]{3,2,0,1:T(8,128)}, f32[12,1,32,512]{3,2,0,1:T(8,128)}), (f32[12,1,32,512]{3,2,0,1:T(8,128)}, f32[12,1,32,512]{3,2,0,1:T(8,128)})) %all-reduce.8.cloned.1.call-update) | async-done | bytes 1572880 | tf_op jit(solution)/shard_map/psum | solution.py:12
  411.1 1.5 pad_maximum_fusion
  413.0 1.1 copy-done.4
  414.0 3.9 convolution_subtract_fusion.1
  418.1 24.8 %all_gather.14 = f32[384,512]{0,1:T(8,128)S(1)} all-gather(f32[384,32]{0,1:T(8,128)S(1)} %copy.47), channel_id=1, replica_groups=mesh['row'=32,'col'=16] {'col'}, dimensions={1}, use_global_device_ids=true | all-gather | bytes 835584 | tf_op jit(solution)/shard_map/all_gather | solution.py:35
  443.0 0.9 copy-done.1
  443.9 0.7 copy.48
  444.9 73.2 %all-gather.5.cloned.1.call-done = f32[1024,512]{1,0:T(8,128)} async-done(((f32[32,512]{1,0:T(8,128)}), f32[1024,512]{1,0:T(8,128)}) %all-gather.5.cloned.1.call-update) | async-done | bytes 2097168 | tf_op jit(solution)/shard_map/all_gather | solution.py:36
  518.1 2.3 slice.135
  520.4 1.6 copy.57
  521.9 1.4 fusion
  523.4 1.0 copy-done.3
  524.4 11.7 %cholesky.358 = f32[128,128]{1,0:T(8,128)S(1)} custom-call(f32[128,128]{1,0:T(8,128)S(1)} %cholesky.439), custom_call_target="Cholesky" | custom-call | tf_op jit(solution)/shard_map/jit(cholesky)/cholesky | solution.py:37
  536.8 9.8 %custom-call.31 = f32[1,128,128]{1,2,0:T(8,128)S(1)} custom-call(f32[1,128,128]{2,1,0:T(8,128)S(1)} %get-tuple-element.60), custom_call_target="InvertDiagBlocksLowerTriangular" | custom-call | tf_op jit(solution)/shard_map/jit(cholesky)/cholesky | solution.py:37
  546.8 1.2 constant_dynamic-update-slice_fusion.3
  548.0 1.3 convolution_subtract_fusion.5
  549.3 11.7 %cholesky.377 = f32[128,128]{1,0:T(8,128)S(1)} custom-call(f32[128,128]{1,0:T(8,128)S(1)} %cholesky.443), custom_call_target="Cholesky" | custom-call | tf_op jit(solution)/shard_map/jit(cholesky)/cholesky | solution.py:37
  561.7 10.0 %custom-call.32 = f32[1,128,128]{1,2,0:T(8,128)S(1)} custom-call(f32[1,128,128]{2,1,0:T(8,128)S(1)} %get-tuple-element.57), custom_call_target="InvertDiagBlocksLowerTriangular" | custom-call | tf_op jit(solution)/shard_map/jit(cholesky)/cholesky | solution.py:37
  571.9 1.3 convolution_subtract_fusion.10
  573.2 11.7 %cholesky.398 = f32[128,128]{1,0:T(8,128)S(1)} custom-call(f32[128,128]{1,0:T(8,128)S(1)} %cholesky.448), custom_call_target="Cholesky" | custom-call | tf_op jit(solution)/shard_map/jit(cholesky)/cholesky | solution.py:37
  585.7 9.8 %custom-call.33 = f32[1,128,128]{1,2,0:T(8,128)S(1)} custom-call(f32[1,128,128]{2,1,0:T(8,128)S(1)} %get-tuple-element.54), custom_call_target="InvertDiagBlocksLowerTriangular" | custom-call | tf_op jit(solution)/shard_map/jit(cholesky)/cholesky | solution.py:37
  595.7 1.2 convolution_subtract_fusion.12
  596.9 11.7 %cholesky.415 = f32[128,128]{1,0:T(8,128)S(1)} custom-call(f32[128,128]{1,0:T(8,128)S(1)} %convolution_subtract_fusion.12), custom_call_target="Cholesky" | custom-call | tf_op jit(solution)/shard_map/jit(cholesky)/cholesky | solution.py:37
  608.7 0.9 compare_reduce_fusion
  612.1 1.1 select_select_fusion
  613.2 11.7 %while.5 = (s32[]{:T(128)}, f32[512,512]{1,0:T(8,128)}, s32[4,2]{0,1:T(2,128)S(1)}, f32[4,128,128]{2,1,0:T(8,128)S(1)}, s32[]{:T(128)}) while((s32[]{:T(128)}, f32[512,512]{1,0:T(8,128)}, s32[4,2]{0,1:T(2,128)S(1)}, f32[4,128,128]{2,1,0:T(8,128)S(1)}, s32[]{:T(128)}) %tuple.71), condition=%wide.while_cond.clone, body=%wide.while_body.clone.sunk | while | flops 2 | bytes 131189 | solution.py:38
  613.9 2.2 bitcast_dynamic-update-slice_fusion.5
  616.8 2.2 bitcast_dynamic-update-slice_fusion.5
  619.8 2.2 bitcast_dynamic-update-slice_fusion.5
  622.7 2.2 bitcast_dynamic-update-slice_fusion.5
  624.9 39.3 %custom-call.34 = f32[4,128,128]{1,2,0:T(8,128)S(1)} custom-call(f32[4,128,128]{2,1,0:T(8,128)S(1)} %get-tuple-element.22), custom_call_target="InvertDiagBlocksLowerTriangular" | custom-call | tf_op jit(solution)/shard_map/jit(_solve_triangular)/triangular_solve | solution.py:38
  664.2 1.3 fusion.27
  665.6 1.2 convolution_subtract_fusion.4
  667.1 1.3 convolution_subtract_fusion.3
  668.8 1.5 convolution_subtract_fusion.2
  670.8 1.2 copy.51
  672.0 1.2 copy.52
  673.3 1.4 slice.132
  674.9 158.1 %all-reduce.6.cloned.1.call-done = (f32[12,1,32,512]{3,2,0,1:T(8,128)}, f32[12,1,32,512]{3,2,0,1:T(8,128)}) async-done(((f32[12,1,32,512]{3,2,0,1:T(8,128)}, f32[12,1,32,512]{3,2,0,1:T(8,128)}), (f32[12,1,32,512]{3,2,0,1:T(8,128)}, f32[12,1,32,512]{3,2,0,1:T(8,128)})) %all-reduce.6.cloned.1.call-update) | async-done | bytes 1572880 | tf_op jit(solution)/shard_map/psum | solution.py:12
  833.0 1.5 pad_maximum_fusion.1
  834.9 1.1 copy-done
  835.9 4.1 convolution_subtract_fusion
  840.4 1.5 pad_maximum_fusion.2
  (99 shorter events, 19.4 us)
Async XLA Ops:
  6.5 104.7 %all-gather.3.cloned.1.call-start = ((), (), s32[]{:S(2)}) async-start(), calls=%async_computation | async-start | bytes 2162688 | tf_op jit(solution)/shard_map/all_gather | solution.py:36
  35.0 376.1 %all-reduce.8.cloned.1.call-start = ((), (), s32[]{:S(2)}) async-start(), calls=%async_computation.3 | async-start | bytes 3145728 | tf_op jit(solution)/shard_map/psum | solution.py:12
  111.3 1.2 slice-start
  251.2 266.9 %all-gather.5.cloned.1.call-start = ((), (), s32[]{:S(2)}) async-start(), calls=%async_computation.1 | async-start | bytes 2162688 | tf_op jit(solution)/shard_map/all_gather | solution.py:36
  412.8 1.3 copy-start.4
  443.0 0.9 copy-start.1
  444.7 388.3 %all-reduce.6.cloned.1.call-start = ((), (), s32[]{:S(2)}) async-start(), calls=%async_computation.2 | async-start | bytes 3145728 | tf_op jit(solution)/shard_map/psum | solution.py:12
  523.4 1.0 copy-start.3
  613.2 52.4 %copy-start.2 = (f32[384,512]{0,1:T(8,128)S(1)}, f32[384,512]{0,1:T(8,128)}, u32[]{:S(2)}) copy-start(f32[384,512]{0,1:T(8,128)} %copy-done.1) | copy-start | bytes 2359300
  834.7 1.3 copy-start
Sparse Core Ops, SparseCore 0:
  35.1 76.0 all-gather.2
  251.4 159.6 all-reduce.7
  444.8 73.2 all-gather.4
  673.3 159.6 all-reduce.5
where the time goes:
time: 861 us; the launch traced here: 849 us
  waiting for transfers between devices  467 us (54%)
  other arithmetic  247 us (29%)
  blocking collectives  51.5 us (6%)
  local copies, waits for them, and re-layouts  39.5 us (5%)
  matrix products  24.4 us (3%)
  between operations  19.2 us (2%)
    psum x2, waiting for transfers between devices, spread(): return lax.psum(block, axis)  318 us
    another operation x29, other arithmetic, shards(): factor = jnp.linalg.cholesky(stacked[start_col:end_col])  158 us
    all_gather x2, waiting for transfers between devices, shards(): stacked = lax.all_gather(columns[0:block_width], 'row', axis=0, tiled=True)  149 us
    another operation x5, other arithmetic, shards(): solved = jax.scipy.linalg.solve_triangular(factor, columns.T, lower=True).T  80.3 us
    all_gather x2, blocking collectives, shards(): columns = lax.all_gather(thin_slice, 'col', axis=1, tiled=True)  51.5 us
    another operation x27, local copies, waits for them, and re-layouts, shards(): solved = jax.scipy.linalg.solve_triangular(factor, columns.T, lower=True).T  20.1 us
  transfers between devices with their start and end apart: 4, of which 4 were waited for; matrix products, arithmetic and copies ran while one was open for 0% of the time, Pallas kernels for 0%

commit v1 on v0

v1 whole, which is shorter than its diff:
```python
import jax
import jax.numpy as jnp
from jax import lax
from jax.experimental import pallas as pl
from jax.experimental.pallas import tpu as pltpu
from jax.sharding import Mesh
from jax.sharding import PartitionSpec as P

NB = 512
PANELS = 2
BS = 32
PR = NB * PANELS
B = 128
KB = PR // B

f32 = jnp.float32
bf16 = jnp.bfloat16
NN = (((1,), (0,)), ((), ()))
NT = (((1,), (1,)), ((), ()))


def split(x):
    hi = x.astype(bf16)
    lo = (x - hi.astype(f32)).astype(bf16)
    return hi, lo


def dot(a, b, dims):
    return lax.dot_general(a, b, dims, preferred_element_type=f32)


def dot3(a, b, dims):
    ah, al = a
    bh, bl = b
    return dot(ah, bh, dims) + (dot(ah, bl, dims) + dot(al, bh, dims))


def tree(terms):
    while len(terms) > 1:
        terms = [sum(terms[i : i + 2][1:], terms[i]) for i in range(0, len(terms), 2)]
    return terms[0]


def lane_b(x, lane):
    return jnp.broadcast_to(x[:, lane : lane + 1], (8, 128))


def sub_b(x, row):
    return jnp.broadcast_to(x[row : row + 1, :], (8, 128))


def factor128(d_ref, y_ref, g_ref, lbt_ref, fill):
    row = lax.broadcasted_iota(jnp.int32, (8, 128), 0)
    lane = lax.broadcasted_iota(jnp.int32, (8, 128), 1)
    S = [d_ref[8 * s : 8 * s + 8, :] for s in range(16)]
    G = [jnp.where(lane == row + 8 * s, 1.0, 0.0).astype(f32) for s in range(16)]

    def column(vals):
        v = vals[7]
        for t in range(6, -1, -1):
            v = jnp.where(row == t, vals[t], v)
        return v

    for s in range(16):
        c = [lane_b(S[s], 8 * s + m) for m in range(8)]
        a = {(t, m): sub_b(c[m], t) for m in range(8) for t in range(m, 8)}
        M = {}
        d = []
        for i in range(8):
            pivot = a[i, i]
            p = 1.0 / pivot
            d.append(pivot)
            old = {j: a[max(i, j), min(i, j)] for j in range(8) if j != i}
            scaled = {j: old[j] * p for j in old}
            for j in old:
                if j > i:
                    M[j, i] = scaled[j]
            for k in old:
                for j in old:
                    if j <= k:
                        a[k, j] = a[k, j] - old[j] * scaled[k]
            for j in old:
                a[max(i, j), min(i, j)] = scaled[j]
            a[i, i] = -p
        w = [column([a[max(t, m), min(t, m)] for t in range(8)]) for m in range(8)]
        YS = tree([w[m] * sub_b(S[s], m) for m in range(8)])
        YG = tree([w[m] * sub_b(G[s], m) for m in range(8)])
        y_ref[8 * s : 8 * s + 8, :] = -YG
        g_ref[8 * s : 8 * s + 8, :] = G[s]
        ys = [sub_b(YS, m) for m in range(8)]
        yg = [sub_b(YG, m) for m in range(8)]
        for r in range(s + 1, 16):
            b = [lane_b(S[r], 8 * s + m) for m in range(8)]
            S[r] = S[r] + tree([b[m] * ys[m] for m in range(8)])
            G[r] = G[r] + tree([b[m] * yg[m] for m in range(8)])
        sq = [jnp.sqrt(d[i]) for i in range(8)]
        zero = jnp.zeros((8, 128), f32)
        lb = zero
        for t in range(8):
            vals = [M[t, i] * sq[i] for i in range(t)] + [sq[t]] + [zero] * (7 - t)
            lb = jnp.where(lane == 8 * s + t, column(vals), lb)
        lbt_ref[8 * s : 8 * s + 8, :] = lb
        fill(s)


def factor_and_update(ids, gathered, a_cols, local):
    RR, CC = local.shape
    W = PR + RR + CC
    n_col = PR // (PANELS * BS)

    def kern(id_ref, pr_ref, ac, al, out, E, D, Y, G, LBT, YQ, GQ, LQ, LT, RHH, RLO, LRH, LRL, ZCH, ZCL, XT):
        for c in range(n_col):
            for p in range(PANELS):
                src = (c * PANELS + p) * BS
                dst = p * NB + c * BS
                E[dst : dst + BS, 0 : PR + RR] = pr_ref[src : src + BS, :]
        E[:, PR + RR :] = ac[...]
        D[...] = E[0:B, 0:B]
        for ref in (YQ, GQ, LQ):
            ref[...] = jnp.zeros(ref.shape, bf16)
        rid = id_ref[0]
        cid = id_ref[1]
        second = rid >= NB // BS
        lane_r = lax.broadcasted_iota(jnp.int32, (B, RR), 1)

        def panel_chunks(q, q0, with_p):
            def eq(c0, w):
                return split(E[pl.ds(q0, B), c0 : c0 + w])

            def yq():
                return YQ[0], YQ[1]

            def gq():
                return GQ[0], GQ[1]

            def keep(c0, w, h, l):
                RHH[0:B, c0 : c0 + w] = h
                RHH[B : 2 * B, c0 : c0 + w] = h
                RLO[:, c0 : c0 + w] = l

            def row_panel(c0, w):
                def f():
                    h, l = split(dot3(yq(), eq(c0, w), NN))
                    keep(c0, w, h, l)
                    if c0 >= PR + RR:
                        cc = c0 - PR - RR
                        ZCH[pl.ds(q0, B), cc : cc + w] = h
                        ZCL[pl.ds(q0, B), cc : cc + w] = l

                return f

            def r_panel():
                e = eq(PR, RR)
                zp = split(dot3(yq(), e, NN))
                keep(PR, RR, *zp)
                XT[pl.ds(q0, B), :] = dot3((LQ[0], LQ[1]), zp, NN)
                zr = dot3(gq(), e, NN)
                live = jnp.logical_and(second, q < NB // B)
                zr = jnp.where(jnp.logical_and(lane_r < BS, jnp.logical_not(live)), 0.0, zr)
                h, l = split(zr.T)
                LRH[:, pl.ds(q0, B)] = h
                LRL[:, pl.ds(q0, B)] = l

            def col_panel(j):
                def f():
                    e = split(E[j * B : (j + 1) * B, pl.ds(q0, B)])
                    h, l = split(dot3(e, gq(), NT))
                    LT[j * B : (j + 1) * B, 0:B] = h
                    LT[j * B : (j + 1) * B, B : 2 * B] = l

                return f

            chunks = []
            if with_p:
                chunks += [col_panel(j) for j in range(KB)]
                chunks += [row_panel(c0, 256) for c0 in range(0, PR, 256)]
            chunks += [row_panel(c0, 256) for c0 in range(PR + RR, W, 256)]
            return chunks + [r_panel]

        def trail_chunks():
            def trail(j, c0, w):
                def f():
                    rows = slice(j * B, (j + 1) * B)
                    u = dot(LT[rows, :], RHH[:, c0 : c0 + w], NN)
                    u = u + dot(LT[rows, 0:B], RLO[:, c0 : c0 + w], NN)
                    E[rows, c0 : c0 + w] = E[rows, c0 : c0 + w] - u

                return f

            parts = ((0, 512), (512, 512), (PR, RR), (PR + RR, CC))
            return [trail(j, c0, w) for j in range(KB) for c0, w in parts]

        def body(k, carry):
            q = jnp.maximum(k - 1, 0)
            q0 = pl.multiple_of(q * B, B)
            k0 = pl.multiple_of(k * B, B)
            n0 = pl.multiple_of(jnp.minimum(k + 1, KB - 1) * B, B)
            chunks = panel_chunks(q, q0, True) + trail_chunks()
            n = len(chunks)

            def fill(s):
                for f in chunks[n * s // 16 : n * (s + 1) // 16]:
                    f()

            factor128(D, Y, G, LBT, fill)
            y = split(Y[...])
            g = split(G[...])
            lb = split(LBT[...])
            for i in range(2):
                YQ[i] = y[i]
                GQ[i] = g[i]
                LQ[i] = lb[i]
            zp = split(dot3(y, split(E[pl.ds(k0, B), pl.ds(n0, B)]), NN))
            zt = split(dot3(split(E[pl.ds(n0, B), pl.ds(k0, B)]), g, NT))
            D[...] = E[pl.ds(n0, B), pl.ds(n0, B)] - dot3(zt, zp, NN)
            return carry

        lax.fori_loop(0, KB, body, 0)
        for f in panel_chunks(KB - 1, (KB - 1) * B, False):
            f()
        for c0 in range(0, CC, 256):
            zh = ZCH[:, c0 : c0 + 256]
            zl = ZCL[:, c0 : c0 + 256]
            u = dot(LRH[...], zh, NN) + (dot(LRH[...], zl, NN) + dot(LRL[...], zh, NN))
            out[:, c0 : c0 + 256] = al[:, c0 : c0 + 256] - u
        for p in range(PANELS):
            c0 = pl.multiple_of(cid * BS + p * NB, BS)
            x = XT[pl.ds(c0, BS), :]
            col = c0 + lax.broadcasted_iota(jnp.int32, (BS, RR), 0)
            ln = lax.broadcasted_iota(jnp.int32, (BS, RR), 1)
            x = jnp.where(jnp.logical_and(ln < BS, col > rid * BS + ln), 0.0, x)
            out[:, BS * p : BS * (p + 1)] = x.T

    vm = pl.BlockSpec(memory_space=pltpu.VMEM)
    V = pltpu.VMEM
    return pl.pallas_call(
        kern,
        out_shape=jax.ShapeDtypeStruct((RR, CC), f32),
        in_specs=[pl.BlockSpec(memory_space=pltpu.SMEM)] + [vm] * 3,
        out_specs=vm,
        scratch_shapes=[
            V((PR, W), f32),
            V((B, B), f32),
            V((B, B), f32),
            V((B, B), f32),
            V((B, B), f32),
            V((2, B, B), bf16),
            V((2, B, B), bf16),
            V((2, B, B), bf16),
            V((PR, 2 * B), bf16),
            V((2 * B, W), bf16),
            V((B, W), bf16),
            V((RR, PR), bf16),
            V((RR, PR), bf16),
            V((PR, CC), bf16),
            V((PR, CC), bf16),
            V((PR, RR), f32),
        ],
        compiler_params=pltpu.CompilerParams(vmem_limit_bytes=40 * 1024 * 1024),
        name="factor_and_update",
    )(ids, gathered, a_cols, local)


def shards(matrix):
    rid = lax.axis_index(("y", "x"))
    cid = lax.axis_index(("z", "k"))
    ids = jnp.stack([rid, cid]).astype(jnp.int32)
    n_row = lax.axis_size(("y", "x"))
    thin = PANELS * BS
    a_cols = lax.all_gather(matrix[:BS], "x", axis=0, tiled=True)
    a_cols = lax.all_gather(a_cols, "y", axis=0, tiled=True)
    block = matrix[:BS, :thin].reshape(1, BS * thin // 128, 128)
    block = jnp.broadcast_to(block, (n_row, BS * thin // 128, 128))
    own = lax.all_to_all(block, ("y", "x"), 0, 0, tiled=True).reshape(PR, thin).T
    mine = jnp.concatenate([own, matrix[:, :thin].T], axis=1)
    gathered = lax.all_gather(mine, ("z", "k"), axis=0, tiled=True)
    return factor_and_update(ids, gathered, a_cols, matrix)


def solution(mesh):
    four = Mesh(mesh.devices.reshape(8, 4, 8, 2), ("y", "x", "z", "k"))
    placed = P(("y", "x"), ("z", "k"))
    return jax.shard_map(shards, mesh=four, in_specs=(placed,), out_specs=placed, check_vma=False)
```

time: 861 us -> 189 us (0.22); the launches traced: 849 us -> 188 us
  waiting for transfers between devices: 467 us -> 91.6 us
  other arithmetic: 247 us -> 0.84 us
  Pallas kernels: 0 us -> 53.4 us
  blocking collectives: 51.5 us -> 11.5 us
  local copies, waits for them, and re-layouts: 39.5 us -> 8.42 us
  matrix products: 24.4 us -> 0 us
  starting transfers between devices: 0.3 us -> 9.1 us
    psum x2 -> x0, waiting for transfers between devices: 318 us -> none  [spread(): return lax.psum(block, axis)]
    another operation x36 -> x1, other arithmetic: 241 us -> 0.08 us  [shards(): ids = jnp.stack([rid, cid]).astype(jnp.int32)]
    all_gather x2, waiting for transfers between devices: 149 us -> 82.3 us  [the longest x1 50.1 us: shards(): gathered = lax.all_gather(mine, ('z', 'k'), axis=0, tiled=True)]
    pallas_call x0 -> x1, Pallas kernels: none -> 53.4 us  [factor_and_update(): pl.pallas_call(kern, out_shape=jax.ShapeDtypeStruct((RR, CC), f32), in_sp...]
    all_gather x2 -> x1, blocking collectives: 51.5 us -> 11.5 us  [shards(): a_cols = lax.all_gather(matrix[:BS], 'x', axis=0, tiled=True)]
    another operation x37 -> x0, local copies, waits for them, and re-layouts: 20.6 us -> none  [the longest x27 20.1 us: shards(): solved = jax.scipy.linalg.solve_triangular(factor, columns.T, lower=True).T]
    another operation x26 -> x0, matrix products: 16.4 us -> none  [the longest x14 9.1 us: shards(): solved = jax.scipy.linalg.solve_triangular(factor, columns.T, lower=True).T]
    all_to_all x0 -> x1, waiting for transfers between devices: none -> 9.29 us  [shards(): lax.all_to_all(block, ('y', 'x'), 0, 0, tiled=True).reshape(PR, thin)]
  transfers between devices with their start and end apart: 4 -> 3, of which waited for: 4 -> 3; matrix products, arithmetic and copies ran while one was open for 0% -> 2% of each run, Pallas kernels for 0% -> 0%
where the time goes in v1:
time: 189 us; the launch traced here: 188 us
  waiting for transfers between devices  91.6 us (48%)
  Pallas kernels  53.4 us (28%)
  between operations  13.4 us (7%)
  blocking collectives  11.5 us (6%)
  starting transfers between devices  9.1 us (5%)
  local copies, waits for them, and re-layouts  8.42 us (4%)
    pallas_call x1, Pallas kernels, factor_and_update(): pl.pallas_call(kern, out_shape=jax.ShapeDtypeStruct((RR, CC), f32), in_sp...  53.4 us
    all_gather x1, waiting for transfers between devices, shards(): gathered = lax.all_gather(mine, ('z', 'k'), axis=0, tiled=True)  50.1 us
    all_gather x1, waiting for transfers between devices, shards(): a_cols = lax.all_gather(a_cols, 'y', axis=0, tiled=True)  32.2 us
    all_gather x1, blocking collectives, shards(): a_cols = lax.all_gather(matrix[:BS], 'x', axis=0, tiled=True)  11.5 us
    all_to_all x1, waiting for transfers between devices, shards(): lax.all_to_all(block, ('y', 'x'), 0, 0, tiled=True).reshape(PR, thin)  9.29 us
    all_to_all x1, starting transfers between devices, shards(): lax.all_to_all(block, ('y', 'x'), 0, 0, tiled=True).reshape(PR, thin)  9.05 us
    unnamed x7, local copies, waits for them, and re-layouts  4.64 us
  transfers between devices with their start and end apart: 3, of which 3 were waited for; matrix products, arithmetic and copies ran while one was open for 2% of the time, Pallas kernels for 0%

profile of v1, /device:TPU:1, one launch (start us, length us, event | category | flops | bytes accessed | tf_op | source)
XLA Modules:
  0.0 188.4 jit_solution(3204775363539680081)
XLA Ops:
  6.5 0.0 copy-start.2
  6.5 0.0 all-gather.5.cloned.1.call-start
  6.5 1.0 slice.11
  7.5 11.5 %all_gather.10 = f32[128,768]{1,0:T(8,128)} all-gather(f32[32,768]{1,0:T(8,128)S(1)} %slice.11), channel_id=1, replica_groups=mesh['y'=8,'x'=4,'z'=8,'k'=2] {'x'}, dimensions={0}, use_global_device_ids=true | all-gather | bytes 491520 | tf_op jit(solution)/shard_map/all_gather | solution.py:270
  19.1 0.0 all-gather.5.cloned.1.call-update
  19.1 0.7 slice.9
  19.8 0.1 broadcast_in_dim.7
  19.9 0.7 broadcast_in_dim.8
  20.6 9.1 %all-to-all-start = ((f32[32,16,128]{2,1,0:T(8,128)}), f32[32,16,128]{2,1,0:T(8,128)S(1)}, u32[]{:S(2)}, u32[]{:S(2)}) async-start(f32[32,16,128]{2,1,0:T(8,128)} %broadcast_in_dim.8), calls=%async_computation | async-start | bytes 524288 | tf_op jit(solution)/shard_map/all_to_all | solution.py:274
  29.7 0.0 all-gather.3.cloned.1.call-start
  29.7 0.9 slice.10
  30.7 0.1 copy.5
  30.8 9.3 %all-to-all-done = f32[32,16,128]{2,1,0:T(8,128)S(1)} async-done(((f32[32,16,128]{2,1,0:T(8,128)}), f32[32,16,128]{2,1,0:T(8,128)S(1)}, u32[]{:S(2)}, u32[]{:S(2)}) %all-to-all-start) | async-done | bytes 262176 | tf_op jit(solution)/shard_map/all_to_all | solution.py:274
  40.1 0.1 reshape.5
  40.2 0.2 copy.3
  40.4 0.8 pad_maximum_fusion
  41.2 0.0 all-gather.3.cloned.1.call-update
  41.2 0.1 pad_add_fusion.id_ref
  41.3 32.2 %all-gather.5.cloned.1.call-done.ac = f32[1024,768]{1,0:T(8,128)} async-done(((f32[128,768]{1,0:T(8,128)}), f32[1024,768]{1,0:T(8,128)}) %all-gather.5.cloned.1.call-update) | async-done | bytes 3145744 | tf_op jit(solution)/shard_map/all_gather | solution.py:271
  73.5 50.1 %all-gather.3.cloned.1.call-done.pr_ref = f32[1024,1408]{1,0:T(8,128)} async-done(((f32[64,1408]{1,0:T(8,128)}), f32[1024,1408]{1,0:T(8,128)}) %all-gather.3.cloned.1.call-update) | async-done | bytes 5767184 | tf_op jit(solution)/shard_map/all_gather | solution.py:276
  123.6 0.0 copy-done.2
  123.6 0.0 copy-start
  123.6 2.6 %copy-done = f32[1024,1408]{1,0:T(8,128)S(1)} copy-done((f32[1024,1408]{1,0:T(8,128)S(1)}, f32[1024,1408]{1,0:T(8,128)}, u32[]{:S(2)}) %copy-start) | copy-done | bytes 5767192
  126.2 0.0 copy-start.1
  126.3 1.9 %copy-done.1 = f32[1024,768]{1,0:T(8,128)S(1)} copy-done((f32[1024,768]{1,0:T(8,128)S(1)}, f32[1024,768]{1,0:T(8,128)}, u32[]{:S(2)}) %copy-start.1) | copy-done | bytes 3145752
  128.1 53.4 %factor_and_update.1 = f32[384,768]{1,0:T(8,128)} custom-call(s32[2]{0:T(128)S(1)} %pad_add_fusion.id_ref, f32[1024,1408]{1,0:T(8,128)S(1)} %copy-done, f32[1024,768]{1,0:T(8,128)S(1)} %copy-done.1, f32[384,768]{1,0:T(8,128)S(1)} %copy-done.2), custom_call_target="tpu_custom_call" | custom-call | tf_op jit(solution)/shard_map/factor_and_update/pallas_call | solution.py:236
Async XLA Ops:
  6.5 117.1 %copy-start.2 = (f32[384,768]{1,0:T(8,128)S(1)}, f32[384,768]{1,0:T(8,128)}, u32[]{:S(2)}) copy-start(f32[384,768]{1,0:T(8,128)} %al.1) | copy-start | bytes 3538948
  6.5 67.0 %all-gather.5.cloned.1.call-start = ((), (), s32[]{:S(2)}) async-start(), calls=%async_computation.2 | async-start | bytes 3538944 | tf_op jit(solution)/shard_map/all_gather | solution.py:271
  20.6 19.5 %all-to-all-start = ((f32[32,16,128]{2,1,0:T(8,128)}), f32[32,16,128]{2,1,0:T(8,128)S(1)}, u32[]{:S(2)}, u32[]{:S(2)}) async-start(f32[32,16,128]{2,1,0:T(8,128)} %broadcast_in_dim.8), calls=%async_computation | async-start | bytes 524288 | tf_op jit(solution)/shard_map/all_to_all | solution.py:274
  29.7 93.9 %all-gather.3.cloned.1.call-start = ((), (), s32[]{:S(2)}) async-start(), calls=%async_computation.1 | async-start | bytes 6127616 | tf_op jit(solution)/shard_map/all_gather | solution.py:276
  123.6 2.6 %copy-start = (f32[1024,1408]{1,0:T(8,128)S(1)}, f32[1024,1408]{1,0:T(8,128)}, u32[]{:S(2)}) copy-start(f32[1024,1408]{1,0:T(8,128)} %all-gather.3.cloned.1.call-done.pr_ref) | copy-start | bytes 17301508
  126.2 1.9 %copy-start.1 = (f32[1024,768]{1,0:T(8,128)S(1)}, f32[1024,768]{1,0:T(8,128)}, u32[]{:S(2)}) copy-start(f32[1024,768]{1,0:T(8,128)} %all-gather.5.cloned.1.call-done.ac) | copy-start | bytes 9437188
Sparse Core Ops, SparseCore 0:
  19.2 54.2 all-gather.4
  75.6 47.9 all-gather.2

commit v2 on v1

--- a/solution.py
+++ b/solution.py
@@ -103,30 +103,45 @@
         fill(s)
 
 
-def factor_and_update(ids, gathered, a_cols, local):
-    RR, CC = local.shape
-    W = PR + RR + CC
+def drain(chunks):
+    for f in chunks:
+        f()
+
+
+def crit(E, D, Y, G, k0, n0):
+    zp = split(dot3(Y, split(E[pl.ds(k0, B), pl.ds(n0, B)]), NN))
+    zt = split(dot3(split(E[pl.ds(n0, B), pl.ds(k0, B)]), G, NT))
+    D[...] = E[pl.ds(n0, B), pl.ds(n0, B)] - dot3(zt, zp, NN)
+
+
+def panel_solve(ids, gathered):
+    W = gathered.shape[1]
+    RR = W - PR
     n_col = PR // (PANELS * BS)
 
-    def kern(id_ref, pr_ref, ac, al, out, E, D, Y, G, LBT, YQ, GQ, LQ, LT, RHH, RLO, LRH, LRL, ZCH, ZCL, XT):
+    def kern(id_ref, pr_ref, vth, vtl, xc, E, D, Y, G, LBT, YQ, GQ, LQ, LT, RHH, RLO, ZPH, ZPL, ZR, GTH, GTL, VH, VL, XT, sems):
+        copies = []
         for c in range(n_col):
             for p in range(PANELS):
-                src = (c * PANELS + p) * BS
-                dst = p * NB + c * BS
-                E[dst : dst + BS, 0 : PR + RR] = pr_ref[src : src + BS, :]
-        E[:, PR + RR :] = ac[...]
-        D[...] = E[0:B, 0:B]
+                n = c * PANELS + p
+                copies.append(
+                    pltpu.make_async_copy(
+                        pr_ref.at[pl.ds(n * BS, BS), :], E.at[pl.ds(p * NB + c * BS, BS), :], sems.at[n]
+                    )
+                )
+        for copy in copies:
+            copy.start()
         for ref in (YQ, GQ, LQ):
             ref[...] = jnp.zeros(ref.shape, bf16)
+        for copy in copies:
+            copy.wait()
+        D[...] = E[0:B, 0:B]
         rid = id_ref[0]
         cid = id_ref[1]
         second = rid >= NB // BS
         lane_r = lax.broadcasted_iota(jnp.int32, (B, RR), 1)
 
         def panel_chunks(q, q0, with_p):
-            def eq(c0, w):
-                return split(E[pl.ds(q0, B), c0 : c0 + w])
-
             def yq():
                 return YQ[0], YQ[1]
 
@@ -140,31 +155,29 @@
 
             def row_panel(c0, w):
                 def f():
-                    h, l = split(dot3(yq(), eq(c0, w), NN))
+                    h, l = split(dot3(yq(), split(E[pl.ds(q0, B), c0 : c0 + w]), NN))
                     keep(c0, w, h, l)
-                    if c0 >= PR + RR:
-                        cc = c0 - PR - RR
-                        ZCH[pl.ds(q0, B), cc : cc + w] = h
-                        ZCL[pl.ds(q0, B), cc : cc + w] = l
+                    ZPH[pl.ds(q0, B), c0 : c0 + w] = h
+                    ZPL[pl.ds(q0, B), c0 : c0 + w] = l
 
                 return f
 
             def r_panel():
-                e = eq(PR, RR)
-                zp = split(dot3(yq(), e, NN))
+                z = dot3(yq(), split(E[pl.ds(q0, B), PR:W]), NN)
+                zp = split(z)
                 keep(PR, RR, *zp)
                 XT[pl.ds(q0, B), :] = dot3((LQ[0], LQ[1]), zp, NN)
-                zr = dot3(gq(), e, NN)
                 live = jnp.logical_and(second, q < NB // B)
-                zr = jnp.where(jnp.logical_and(lane_r < BS, jnp.logical_not(live)), 0.0, zr)
-                h, l = split(zr.T)
-                LRH[:, pl.ds(q0, B)] = h
-                LRL[:, pl.ds(q0, B)] = l
+                ZR[pl.ds(q0, B), :] = jnp.where(jnp.logical_and(lane_r < BS, jnp.logical_not(live)), 0.0, z)
+
+            def transposed():
+                h, l = split((gq()[0].astype(f32) + gq()[1].astype(f32)).T)
+                GTH[pl.ds(q0, B), :] = h
+                GTL[pl.ds(q0, B), :] = l
 
             def col_panel(j):
                 def f():
-                    e = split(E[j * B : (j + 1) * B, pl.ds(q0, B)])
-                    h, l = split(dot3(e, gq(), NT))
+                    h, l = split(dot3(split(E[j * B : (j + 1) * B, pl.ds(q0, B)]), gq(), NT))
                     LT[j * B : (j + 1) * B, 0:B] = h
                     LT[j * B : (j + 1) * B, B : 2 * B] = l
 
@@ -174,8 +187,7 @@
             if with_p:
                 chunks += [col_panel(j) for j in range(KB)]
                 chunks += [row_panel(c0, 256) for c0 in range(0, PR, 256)]
-            chunks += [row_panel(c0, 256) for c0 in range(PR + RR, W, 256)]
-            return chunks + [r_panel]
+            return chunks + [r_panel, transposed]
 
         def trail_chunks():
             def trail(j, c0, w):
@@ -187,7 +199,7 @@
 
                 return f
 
-            parts = ((0, 512), (512, 512), (PR, RR), (PR + RR, CC))
+            parts = ((0, 512), (512, 512), (PR, RR))
             return [trail(j, c0, w) for j in range(KB) for c0, w in parts]
 
         def body(k, carry):
@@ -199,8 +211,7 @@
             n = len(chunks)
 
             def fill(s):
-                for f in chunks[n * s // 16 : n * (s + 1) // 16]:
-                    f()
+                drain(chunks[n * s // 16 : n * (s + 1) // 16])
 
             factor128(D, Y, G, LBT, fill)
             y = split(Y[...])
@@ -210,34 +221,40 @@
                 YQ[i] = y[i]
                 GQ[i] = g[i]
                 LQ[i] = lb[i]
-            zp = split(dot3(y, split(E[pl.ds(k0, B), pl.ds(n0, B)]), NN))
-            zt = split(dot3(split(E[pl.ds(n0, B), pl.ds(k0, B)]), g, NT))
-            D[...] = E[pl.ds(n0, B), pl.ds(n0, B)] - dot3(zt, zp, NN)
+            crit(E, D, y, g, k0, n0)
             return carry
 
         lax.fori_loop(0, KB, body, 0)
-        for f in panel_chunks(KB - 1, (KB - 1) * B, False):
-            f()
-        for c0 in range(0, CC, 256):
-            zh = ZCH[:, c0 : c0 + 256]
-            zl = ZCL[:, c0 : c0 + 256]
-            u = dot(LRH[...], zh, NN) + (dot(LRH[...], zl, NN) + dot(LRL[...], zh, NN))
-            out[:, c0 : c0 + 256] = al[:, c0 : c0 + 256] - u
+        drain(panel_chunks(KB - 1, (KB - 1) * B, False))
+        for k in range(KB - 1, -1, -1):
+            rows = slice(k * B, (k + 1) * B)
+            v = ZR[rows, :]
+            if k < KB - 1:
+                later = slice((k + 1) * B, PR)
+                v = v - dot3((ZPH[rows, later], ZPL[rows, later]), (VH[later, :], VL[later, :]), NN)
+            v = dot3((GTH[rows, :], GTL[rows, :]), split(v), NN)
+            h, l = split(v)
+            VH[rows, :] = h
+            VL[rows, :] = l
+            h, l = split(v.T)
+            vth[:, rows] = h
+            vtl[:, rows] = l
         for p in range(PANELS):
             c0 = pl.multiple_of(cid * BS + p * NB, BS)
             x = XT[pl.ds(c0, BS), :]
             col = c0 + lax.broadcasted_iota(jnp.int32, (BS, RR), 0)
             ln = lax.broadcasted_iota(jnp.int32, (BS, RR), 1)
             x = jnp.where(jnp.logical_and(ln < BS, col > rid * BS + ln), 0.0, x)
-            out[:, BS * p : BS * (p + 1)] = x.T
+            xc[:, BS * p : BS * (p + 1)] = x.T
 
     vm = pl.BlockSpec(memory_space=pltpu.VMEM)
     V = pltpu.VMEM
+    out = jax.ShapeDtypeStruct((RR, PR), bf16)
     return pl.pallas_call(
         kern,
-        out_shape=jax.ShapeDtypeStruct((RR, CC), f32),
-        in_specs=[pl.BlockSpec(memory_space=pltpu.SMEM)] + [vm] * 3,
-        out_specs=vm,
+        out_shape=(out, out, jax.ShapeDtypeStruct((RR, PANELS * BS), f32)),
+        in_specs=[pl.BlockSpec(memory_space=pltpu.SMEM), pl.BlockSpec(memory_space=pl.ANY)],
+        out_specs=(vm, vm, vm),
         scratch_shapes=[
             V((PR, W), f32),
             V((B, B), f32),
@@ -250,15 +267,44 @@
             V((PR, 2 * B), bf16),
             V((2 * B, W), bf16),
             V((B, W), bf16),
-            V((RR, PR), bf16),
-            V((RR, PR), bf16),
-            V((PR, CC), bf16),
-            V((PR, CC), bf16),
+            V((PR, PR), bf16),
+            V((PR, PR), bf16),
             V((PR, RR), f32),
+            V((PR, B), bf16),
+            V((PR, B), bf16),
+            V((PR, RR), bf16),
+            V((PR, RR), bf16),
+            V((PR, RR), f32),
+            pltpu.SemaphoreType.DMA((PANELS * n_col,)),
         ],
         compiler_params=pltpu.CompilerParams(vmem_limit_bytes=40 * 1024 * 1024),
-        name="factor_and_update",
-    )(ids, gathered, a_cols, local)
+        cost_estimate=pl.CostEstimate(flops=40_000_000_000, bytes_accessed=8_000_000, transcendentals=0),
+        name="panel_solve",
+    )(ids, gathered)
+
+
+def trailing_update(vth, vtl, xc, a_cols, local):
+    RR, CC = local.shape
+    step = 256
+
+    def kern(vth, vtl, xc, ac, al, out):
+        out[...] = al[...] - dot3((vth[...], vtl[...]), split(ac[...]), NN)
+
+        @pl.when(pl.program_id(0) == 0)
+        def _():
+            out[:, 0 : PANELS * BS] = xc[...]
+
+    whole = lambda a: pl.BlockSpec(a.shape, lambda i: (0, 0))
+    part = lambda rows: pl.BlockSpec((rows, step), lambda i: (0, i))
+    return pl.pallas_call(
+        kern,
+        grid=(CC // step,),
+        out_shape=jax.ShapeDtypeStruct((RR, CC), f32),
+        in_specs=[whole(vth), whole(vtl), whole(xc), part(PR), part(RR)],
+        out_specs=part(RR),
+        compiler_params=pltpu.CompilerParams(vmem_limit_bytes=24 * 1024 * 1024),
+        name="trailing_update",
+    )(vth, vtl, xc, a_cols, local)
 
 
 def shards(matrix):
@@ -267,14 +313,16 @@
     ids = jnp.stack([rid, cid]).astype(jnp.int32)
     n_row = lax.axis_size(("y", "x"))
     thin = PANELS * BS
-    a_cols = lax.all_gather(matrix[:BS], "x", axis=0, tiled=True)
-    a_cols = lax.all_gather(a_cols, "y", axis=0, tiled=True)
     block = matrix[:BS, :thin].reshape(1, BS * thin // 128, 128)
     block = jnp.broadcast_to(block, (n_row, BS * thin // 128, 128))
     own = lax.all_to_all(block, ("y", "x"), 0, 0, tiled=True).reshape(PR, thin).T
     mine = jnp.concatenate([own, matrix[:, :thin].T], axis=1)
+    mine, top = lax.optimization_barrier((mine, matrix[:BS]))
     gathered = lax.all_gather(mine, ("z", "k"), axis=0, tiled=True)
-    return factor_and_update(ids, gathered, a_cols, matrix)
+    a_cols = lax.all_gather(top, "x", axis=0, tiled=True)
+    a_cols = lax.all_gather(a_cols, "y", axis=0, tiled=True)
+    vth, vtl, xc = panel_solve(ids, gathered)
+    return trailing_update(vth, vtl, xc, a_cols, matrix)
 
 
 def solution(mesh):

time: 189 us -> 157 us (0.83)
  waiting for transfers between devices: 91.6 us -> 47.6 us
  Pallas kernels: 53.4 us -> 64.9 us
    all_gather x1, waiting for transfers between devices: 32.2 us -> 0.02 us  [shards(): a_cols = lax.all_gather(a_cols, 'y', axis=0, tiled=True)]
    all_gather x1, waiting for transfers between devices: 50.1 us -> 37.5 us  [shards(): gathered = lax.all_gather(mine, ('z', 'k'), axis=0, tiled=True)]
    pallas_call x1 -> x2, Pallas kernels: 53.4 us -> 64.9 us  [the longest x1 61.5 us: panel_solve(): pl.pallas_call(kern, out_shape=(out, out, jax.ShapeDtypeStruct((RR, PANEL...]
  transfers between devices with their start and end apart: 3 -> 3, of which waited for: 3 -> 2; matrix products, arithmetic and copies ran while one was open for 2% -> 1% of each run, Pallas kernels for 0% -> 39%
where the time goes in v2:
time: 157 us; the launch traced here: 156 us
  Pallas kernels  64.9 us (41%)
  waiting for transfers between devices  47.6 us (30%)
  between operations  13.5 us (9%)
  blocking collectives  11.4 us (7%)
  starting transfers between devices  10.6 us (7%)
  local copies, waits for them, and re-layouts  7.49 us (5%)
    pallas_call x1, Pallas kernels, panel_solve(): pl.pallas_call(kern, out_shape=(out, out, jax.ShapeDtypeStruct((RR, PANEL...  61.5 us
    all_gather x1, waiting for transfers between devices, shards(): gathered = lax.all_gather(mine, ('z', 'k'), axis=0, tiled=True)  37.5 us
    all_gather x1, blocking collectives, shards(): a_cols = lax.all_gather(top, 'x', axis=0, tiled=True)  11.4 us
    all_to_all x1, starting transfers between devices, shards(): lax.all_to_all(block, ('y', 'x'), 0, 0, tiled=True).reshape(PR, thin)  10.5 us
    all_to_all x1, waiting for transfers between devices, shards(): lax.all_to_all(block, ('y', 'x'), 0, 0, tiled=True).reshape(PR, thin)  10.1 us
    unnamed x7, local copies, waits for them, and re-layouts  4.63 us
    pallas_call x1, Pallas kernels, trailing_update(): pl.pallas_call(kern, grid=(CC // step,), out_shape=jax.ShapeDtypeStruct((...  3.44 us
  transfers between devices with their start and end apart: 3, of which 2 were waited for; matrix products, arithmetic and copies ran while one was open for 1% of the time, Pallas kernels for 39%

profile of v2, /device:TPU:1, one launch (start us, length us, event | category | flops | bytes accessed | tf_op | source)
XLA Modules:
  0.0 156.4 jit_solution(7136659300966315992)
XLA Ops:
  6.5 0.0 slice-start
  6.5 0.8 slice.9
  7.3 0.1 broadcast_in_dim.7
  7.4 0.7 broadcast_in_dim.8
  8.1 10.5 %all-to-all-start = ((f32[32,16,128]{2,1,0:T(8,128)}), f32[32,16,128]{2,1,0:T(8,128)S(1)}, u32[]{:S(2)}, u32[]{:S(2)}) async-start(f32[32,16,128]{2,1,0:T(8,128)} %broadcast_in_dim.8), calls=%async_computation | async-start | bytes 524288 | tf_op jit(solution)/shard_map/all_to_all | solution.py:318
  18.6 0.0 all-gather.3.cloned.1.call-start
  18.7 0.9 slice.10
  19.6 0.1 copy.5
  19.7 10.1 %all-to-all-done = f32[32,16,128]{2,1,0:T(8,128)S(1)} async-done(((f32[32,16,128]{2,1,0:T(8,128)}), f32[32,16,128]{2,1,0:T(8,128)S(1)}, u32[]{:S(2)}, u32[]{:S(2)}) %all-to-all-start) | async-done | bytes 262176 | tf_op jit(solution)/shard_map/all_to_all | solution.py:318
  29.8 0.1 reshape.5
  30.0 0.2 copy.3
  30.2 0.8 pad_maximum_fusion
  30.9 0.0 all-gather.3.cloned.1.call-update
  31.0 0.0 all-gather.5.cloned.1.call-start
  31.0 0.0 slice-done
  31.0 11.4 %all_gather.10 = f32[128,768]{1,0:T(8,128)} all-gather(f32[32,768]{1,0:T(8,128)S(1)} %slice-done), channel_id=1, replica_groups=mesh['y'=8,'x'=4,'z'=8,'k'=2] {'x'}, dimensions={0}, use_global_device_ids=true | all-gather | bytes 491520 | tf_op jit(solution)/shard_map/all_gather | solution.py:322
  42.4 0.0 all-gather.5.cloned.1.call-update
  42.5 0.1 pad_add_fusion.id_ref
  42.5 0.0 copy-start.1
  42.6 37.5 %all-gather.3.cloned.1.call-done.pr_ref = f32[1024,1408]{1,0:T(8,128)} async-done(((f32[64,1408]{1,0:T(8,128)}), f32[1024,1408]{1,0:T(8,128)}) %all-gather.3.cloned.1.call-update) | async-done | bytes 5767184 | tf_op jit(solution)/shard_map/all_gather | solution.py:321
  80.1 0.0 copy-start.2
  80.1 2.6 %copy-done.2 = f32[1024,1408]{1,0:T(8,128)S(1)} copy-done((f32[1024,1408]{1,0:T(8,128)S(1)}, f32[1024,1408]{1,0:T(8,128)}, u32[]{:S(2)}) %copy-start.2) | copy-done | bytes 5767192
  82.7 61.5 %panel_solve.1 = (bf16[384,1024]{1,0:T(8,128)(2,1)S(1)}, bf16[384,1024]{1,0:T(8,128)(2,1)S(1)}, f32[384,64]{1,0:T(8,128)S(1)}) custom-call(s32[2]{0:T(128)S(1)} %pad_add_fusion.id_ref, f32[1024,1408]{1,0:T(8,128)S(1)} %copy-done.2), custom_call_target="tpu_custom_call" | custom-call | flops 40000000000 | bytes 8000000 | tf_op jit(solution)/shard_map/panel_solve/pallas_call | solution.py:253
  144.2 0.0 all-gather.5.cloned.1.call-done.ac
  144.2 0.0 copy-done.1
  144.2 0.0 copy-start
  144.2 1.9 %copy-done = f32[1024,768]{1,0:T(8,128)S(1)} copy-done((f32[1024,768]{1,0:T(8,128)S(1)}, f32[1024,768]{1,0:T(8,128)}, u32[]{:S(2)}) %copy-start) | copy-done | bytes 3145752
  146.1 3.4 %trailing_update.1 = f32[384,768]{1,0:T(8,128)} custom-call(bf16[384,1024]{1,0:T(8,128)(2,1)S(1)} %get-tuple-element.11.vth, bf16[384,1024]{1,0:T(8,128)(2,1)S(1)} %get-tuple-element.12.vtl, f32[384,64]{1,0:T(8,128)S(1)} %get-tuple-element.13.xc, f32[1024,768]{1,0:T(8,128)S(1)} %copy-done, f32[384,768]{1,0:T(8,128)S(1)} %copy-done.1), custom_call_target="tpu_custom_call" | custom-call | tf_op jit(solution)/shard_map/trailing_update/pallas_call | solution.py:299
Async XLA Ops:
  6.5 24.5 %slice-start = ((f32[384,768]{1,0:T(8,128)}), f32[32,768]{1,0:T(8,128)S(1)}, s32[]{:S(2)}) async-start(f32[384,768]{1,0:T(8,128)} %al.1), calls=%async_computation.3 | async-start | bytes 196608 | tf_op jit(solution)/shard_map/slice | solution.py:320
  8.1 21.7 %all-to-all-start = ((f32[32,16,128]{2,1,0:T(8,128)}), f32[32,16,128]{2,1,0:T(8,128)S(1)}, u32[]{:S(2)}, u32[]{:S(2)}) async-start(f32[32,16,128]{2,1,0:T(8,128)} %broadcast_in_dim.8), calls=%async_computation | async-start | bytes 524288 | tf_op jit(solution)/shard_map/all_to_all | solution.py:318
  18.6 61.4 %all-gather.3.cloned.1.call-start = ((), (), s32[]{:S(2)}) async-start(), calls=%async_computation.1 | async-start | bytes 6127616 | tf_op jit(solution)/shard_map/all_gather | solution.py:321
  31.0 113.3 %all-gather.5.cloned.1.call-start = ((), (), s32[]{:S(2)}) async-start(), calls=%async_computation.2 | async-start | bytes 3538944 | tf_op jit(solution)/shard_map/all_gather | solution.py:323
  42.5 101.7 %copy-start.1 = (f32[384,768]{1,0:T(8,128)S(1)}, f32[384,768]{1,0:T(8,128)}, u32[]{:S(2)}) copy-start(f32[384,768]{1,0:T(8,128)} %al.1) | copy-start | bytes 3538948
  80.1 2.6 %copy-start.2 = (f32[1024,1408]{1,0:T(8,128)S(1)}, f32[1024,1408]{1,0:T(8,128)}, u32[]{:S(2)}) copy-start(f32[1024,1408]{1,0:T(8,128)} %all-gather.3.cloned.1.call-done.pr_ref) | copy-start | bytes 17301508
  144.2 1.9 %copy-start = (f32[1024,768]{1,0:T(8,128)S(1)}, f32[1024,768]{1,0:T(8,128)}, u32[]{:S(2)}) copy-start(f32[1024,768]{1,0:T(8,128)} %all-gather.5.cloned.1.call-done.ac) | copy-start | bytes 9437188
Sparse Core Ops, SparseCore 0:
  31.1 48.9 all-gather.2
  82.1 44.6 all-gather.4

commit v3 on v2

--- a/solution.py
+++ b/solution.py
@@ -12,6 +12,7 @@
 PR = NB * PANELS
 B = 128
 KB = PR // B
+KA = 2
 
 f32 = jnp.float32
 bf16 = jnp.bfloat16
@@ -56,10 +57,10 @@
     G = [jnp.where(lane == row + 8 * s, 1.0, 0.0).astype(f32) for s in range(16)]
 
     def column(vals):
-        v = vals[7]
-        for t in range(6, -1, -1):
-            v = jnp.where(row == t, vals[t], v)
-        return v
+        for bit in range(3):
+            odd = row // (1 << bit) % 2 == 1
+            vals = [jnp.where(odd, vals[t + 1], vals[t]) for t in range(0, len(vals), 2)]
+        return vals[0]
 
     for s in range(16):
         c = [lane_b(S[s], 8 * s + m) for m in range(8)]
@@ -77,7 +78,9 @@
                     M[j, i] = scaled[j]
             for k in old:
                 for j in old:
-                    if j <= k:
+                    if j == k == i + 1:
+                        a[k, j] = a[k, j] - (old[j] * old[j]) * p
+                    elif j <= k:
                         a[k, j] = a[k, j] - old[j] * scaled[k]
             for j in old:
                 a[max(i, j), min(i, j)] = scaled[j]
@@ -114,12 +117,57 @@
     D[...] = E[pl.ds(n0, B), pl.ds(n0, B)] - dot3(zt, zp, NN)
 
 
-def panel_solve(ids, gathered):
+def first_blocks(a0):
+    N = KA * B
+
+    def kern(a_ref, y0, g0, lbt0, E, D, LT, RHH, RLO):
+        E[...] = a_ref[0:N, :]
+        D[...] = E[0:B, 0:B]
+        for k in range(KA):
+            rows = slice(k * B, (k + 1) * B)
+
+            def fill(s, k=k):
+                if k == 0 or s % 4 or s // 4 >= KA - k:
+                    return
+                j = k + s // 4
+                u = dot(LT[j * B : (j + 1) * B, :], RHH[:, k * B : N], NN)
+                u = u + dot(LT[j * B : (j + 1) * B, 0:B], RLO[:, k * B : N], NN)
+                E[j * B : (j + 1) * B, k * B : N] = E[j * B : (j + 1) * B, k * B : N] - u
+
+            factor128(D, y0.at[rows, :], g0.at[rows, :], lbt0.at[rows, :], fill)
+            if k < KA - 1:
+                y = split(y0[rows, :])
+                g = split(g0[rows, :])
+                crit(E, D, y, g, k * B, (k + 1) * B)
+                h, l = split(dot3(y, split(E[rows, (k + 1) * B : N]), NN))
+                RHH[0:B, (k + 1) * B : N] = h
+                RHH[B : 2 * B, (k + 1) * B : N] = h
+                RLO[:, (k + 1) * B : N] = l
+                h, l = split(dot3(split(E[(k + 1) * B : N, rows]), g, NT))
+                LT[(k + 1) * B : N, 0:B] = h
+                LT[(k + 1) * B : N, B : 2 * B] = l
+
+    vm = pl.BlockSpec(memory_space=pltpu.VMEM)
+    V = pltpu.VMEM
+    out = jax.ShapeDtypeStruct((N, B), f32)
+    return pl.pallas_call(
+        kern,
+        out_shape=(out, out, out),
+        in_specs=[vm],
+        out_specs=(vm, vm, vm),
+        scratch_shapes=[V((N, N), f32), V((B, B), f32), V((N, 2 * B), bf16), V((2 * B, N), bf16), V((B, N), bf16)],
+        compiler_params=pltpu.CompilerParams(vmem_limit_bytes=24 * 1024 * 1024),
+        cost_estimate=pl.CostEstimate(flops=15_000_000_000, bytes_accessed=2_000_000, transcendentals=0),
+        name="first_blocks",
+    )(a0)
+
+
+def panel_solve(ids, gathered, y0, g0, lbt0):
     W = gathered.shape[1]
     RR = W - PR
     n_col = PR // (PANELS * BS)
 
-    def kern(id_ref, pr_ref, vth, vtl, xc, E, D, Y, G, LBT, YQ, GQ, LQ, LT, RHH, RLO, ZPH, ZPL, ZR, GTH, GTL, VH, VL, XT, sems):
+    def kern(id_ref, pr_ref, y0, g0, lbt0, vth, vtl, xc, E, D, Y, G, LBT, YQ, GQ, LQ, LT, RHH, RLO, ZPH, ZPL, LRH, LRL, XT, sems):
         copies = []
         for c in range(n_col):
             for p in range(PANELS):
@@ -131,17 +179,14 @@
                 )
         for copy in copies:
             copy.start()
-        for ref in (YQ, GQ, LQ):
-            ref[...] = jnp.zeros(ref.shape, bf16)
         for copy in copies:
             copy.wait()
-        D[...] = E[0:B, 0:B]
         rid = id_ref[0]
         cid = id_ref[1]
         second = rid >= NB // BS
         lane_r = lax.broadcasted_iota(jnp.int32, (B, RR), 1)
 
-        def panel_chunks(q, q0, with_p):
+        def panel_chunks(q, q0, first):
             def yq():
                 return YQ[0], YQ[1]
 
@@ -162,18 +207,30 @@
 
                 return f
 
+            def pivot_columns():
+                h, l = yq()
+                RHH[0:B, pl.ds(q0, B)] = h
+                RHH[B : 2 * B, pl.ds(q0, B)] = h
+                RLO[:, pl.ds(q0, B)] = l
+                ZPH[pl.ds(q0, B), pl.ds(q0, B)] = h
+                ZPL[pl.ds(q0, B), pl.ds(q0, B)] = l
+                E[first * B : PR, pl.ds(q0, B)] = jnp.zeros((PR - first * B, B), f32)
+
             def r_panel():
-                z = dot3(yq(), split(E[pl.ds(q0, B), PR:W]), NN)
-                zp = split(z)
+                e = split(E[pl.ds(q0, B), PR:W])
+                zp = split(dot3(yq(), e, NN))
                 keep(PR, RR, *zp)
                 XT[pl.ds(q0, B), :] = dot3((LQ[0], LQ[1]), zp, NN)
+                z = dot3(gq(), e, NN)
                 live = jnp.logical_and(second, q < NB // B)
-                ZR[pl.ds(q0, B), :] = jnp.where(jnp.logical_and(lane_r < BS, jnp.logical_not(live)), 0.0, z)
-
-            def transposed():
-                h, l = split((gq()[0].astype(f32) + gq()[1].astype(f32)).T)
-                GTH[pl.ds(q0, B), :] = h
-                GTL[pl.ds(q0, B), :] = l
+                z = jnp.where(jnp.logical_and(lane_r < BS, jnp.logical_not(live)), 0.0, z)
+                h, l = split(z.T)
+                LRH[:, pl.ds(q0, B)] = h
+                LRL[:, pl.ds(q0, B)] = l
+
+            def last_pivot():
+                ZPH[pl.ds(q0, B), pl.ds(q0, B)] = YQ[0]
+                ZPL[pl.ds(q0, B), pl.ds(q0, B)] = YQ[1]
 
             def col_panel(j):
                 def f():
@@ -184,12 +241,11 @@
                 return f
 
             chunks = []
-            if with_p:
-                chunks += [col_panel(j) for j in range(KB)]
-                chunks += [row_panel(c0, 256) for c0 in range(0, PR, 256)]
-            return chunks + [r_panel, transposed]
-
-        def trail_chunks():
+            chunks += [col_panel(j) for j in range(first, KB)]
+            chunks += [row_panel(c0, 256) for c0 in range(0, PR, 256)]
+            return chunks + [pivot_columns, r_panel] if first < KB else chunks + [last_pivot, r_panel]
+
+        def trail_chunks(first):
             def trail(j, c0, w):
                 def f():
                     rows = slice(j * B, (j + 1) * B)
@@ -199,15 +255,23 @@
 
                 return f
 
-            parts = ((0, 512), (512, 512), (PR, RR))
-            return [trail(j, c0, w) for j in range(KB) for c0, w in parts]
+            parts = [(c0, 512) for c0 in range(0, PR, 512)] + [(PR, RR)]
+            return [trail(j, c0, w) for j in range(first, KB) for c0, w in parts]
+
+        for k in range(KA):
+            rows = slice(k * B, (k + 1) * B)
+            for q_ref, ref in ((YQ, y0), (GQ, g0), (LQ, lbt0)):
+                q_ref[0], q_ref[1] = split(ref[rows, :])
+            if k < KA - 1:
+                drain(panel_chunks(k, k * B, k + 1) + trail_chunks(k + 1))
+        crit(E, D, (YQ[0], YQ[1]), (GQ[0], GQ[1]), (KA - 1) * B, KA * B)
 
         def body(k, carry):
-            q = jnp.maximum(k - 1, 0)
+            q = k - 1
             q0 = pl.multiple_of(q * B, B)
             k0 = pl.multiple_of(k * B, B)
             n0 = pl.multiple_of(jnp.minimum(k + 1, KB - 1) * B, B)
-            chunks = panel_chunks(q, q0, True) + trail_chunks()
+            chunks = panel_chunks(q, q0, KA) + trail_chunks(KA)
             n = len(chunks)
 
             def fill(s):
@@ -224,21 +288,15 @@
             crit(E, D, y, g, k0, n0)
             return carry
 
-        lax.fori_loop(0, KB, body, 0)
-        drain(panel_chunks(KB - 1, (KB - 1) * B, False))
-        for k in range(KB - 1, -1, -1):
-            rows = slice(k * B, (k + 1) * B)
-            v = ZR[rows, :]
-            if k < KB - 1:
-                later = slice((k + 1) * B, PR)
-                v = v - dot3((ZPH[rows, later], ZPL[rows, later]), (VH[later, :], VL[later, :]), NN)
-            v = dot3((GTH[rows, :], GTL[rows, :]), split(v), NN)
-            h, l = split(v)
-            VH[rows, :] = h
-            VL[rows, :] = l
-            h, l = split(v.T)
-            vth[:, rows] = h
-            vtl[:, rows] = l
+        lax.fori_loop(KA, KB, body, 0)
+        drain(panel_chunks(KB - 1, (KB - 1) * B, KB))
+        for c0 in range(0, PR, 256):
+            for ref in (ZPH, ZPL):
+                ref[c0 : c0 + B, c0 + B : c0 + 2 * B] = jnp.zeros((B, B), bf16)
+            z = (ZPH[c0:PR, c0 : c0 + 256], ZPL[c0:PR, c0 : c0 + 256])
+            h, l = split(dot3((LRH[:, c0:PR], LRL[:, c0:PR]), z, NN))
+            vth[:, c0 : c0 + 256] = h
+            vtl[:, c0 : c0 + 256] = l
         for p in range(PANELS):
             c0 = pl.multiple_of(cid * BS + p * NB, BS)
             x = XT[pl.ds(c0, BS), :]
@@ -253,7 +311,7 @@
     return pl.pallas_call(
         kern,
         out_shape=(out, out, jax.ShapeDtypeStruct((RR, PANELS * BS), f32)),
-        in_specs=[pl.BlockSpec(memory_space=pltpu.SMEM), pl.BlockSpec(memory_space=pl.ANY)],
+        in_specs=[pl.BlockSpec(memory_space=pltpu.SMEM), pl.BlockSpec(memory_space=pl.ANY), vm, vm, vm],
         out_specs=(vm, vm, vm),
         scratch_shapes=[
             V((PR, W), f32),
@@ -269,18 +327,15 @@
             V((B, W), bf16),
             V((PR, PR), bf16),
             V((PR, PR), bf16),
-            V((PR, RR), f32),
-            V((PR, B), bf16),
-            V((PR, B), bf16),
-            V((PR, RR), bf16),
-            V((PR, RR), bf16),
+            V((RR, PR), bf16),
+            V((RR, PR), bf16),
             V((PR, RR), f32),
             pltpu.SemaphoreType.DMA((PANELS * n_col,)),
         ],
-        compiler_params=pltpu.CompilerParams(vmem_limit_bytes=40 * 1024 * 1024),
-        cost_estimate=pl.CostEstimate(flops=40_000_000_000, bytes_accessed=8_000_000, transcendentals=0),
+        compiler_params=pltpu.CompilerParams(vmem_limit_bytes=58 * 1024 * 1024),
+        cost_estimate=pl.CostEstimate(flops=30_000_000_000, bytes_accessed=8_000_000, transcendentals=0),
         name="panel_solve",
-    )(ids, gathered)
+    )(ids, gathered, y0, g0, lbt0)
 
 
 def trailing_update(vth, vtl, xc, a_cols, local):
@@ -302,7 +357,7 @@
         out_shape=jax.ShapeDtypeStruct((RR, CC), f32),
         in_specs=[whole(vth), whole(vtl), whole(xc), part(PR), part(RR)],
         out_specs=part(RR),
-        compiler_params=pltpu.CompilerParams(vmem_limit_bytes=24 * 1024 * 1024),
+        compiler_params=pltpu.CompilerParams(vmem_limit_bytes=58 * 1024 * 1024),
         name="trailing_update",
     )(vth, vtl, xc, a_cols, local)
 
@@ -317,11 +372,16 @@
     block = jnp.broadcast_to(block, (n_row, BS * thin // 128, 128))
     own = lax.all_to_all(block, ("y", "x"), 0, 0, tiled=True).reshape(PR, thin).T
     mine = jnp.concatenate([own, matrix[:, :thin].T], axis=1)
-    mine, top = lax.optimization_barrier((mine, matrix[:BS]))
+    early = own[:BS, : KA * B]
+    mine, early = lax.optimization_barrier((mine, early))
     gathered = lax.all_gather(mine, ("z", "k"), axis=0, tiled=True)
-    a_cols = lax.all_gather(top, "x", axis=0, tiled=True)
-    a_cols = lax.all_gather(a_cols, "y", axis=0, tiled=True)
-    vth, vtl, xc = panel_solve(ids, gathered)
+    early = lax.all_gather(early, ("z", "k"), axis=0, tiled=True)
+    early, top = lax.optimization_barrier((early, matrix[:BS]))
+    top = lax.all_gather(top, "x", axis=0, tiled=True)
+    early, top = lax.optimization_barrier((early, top))
+    factors = first_blocks(early)
+    a_cols = lax.all_gather(top, "y", axis=0, tiled=True)
+    vth, vtl, xc = panel_solve(ids, gathered, *factors)
     return trailing_update(vth, vtl, xc, a_cols, matrix)
 
 

time: 157 us -> 140 us (0.89)
  waiting for transfers between devices: 47.6 us -> 11 us
  blocking collectives: 11.4 us -> 38.8 us
  Pallas kernels: 64.9 us -> 59.1 us
  local copies, waits for them, and re-layouts: 7.49 us -> 4.91 us
    all_gather x1, waiting for transfers between devices: 37.5 us -> 0.01 us  [shards(): gathered = lax.all_gather(mine, ('z', 'k'), axis=0, tiled=True)]
    all_gather x1 -> x2, blocking collectives: 11.4 us -> 38.8 us  [the longest x1 27.6 us: shards(): early = lax.all_gather(early, ('z', 'k'), axis=0, tiled=True)]
    pallas_call x1, Pallas kernels: 61.5 us -> 43.8 us  [panel_solve(): pl.pallas_call(kern, out_shape=(out, out, jax.ShapeDtypeStruct((RR, PANEL...]
    pallas_call x0 -> x1, Pallas kernels: none -> 9.56 us  [first_blocks(): pl.pallas_call(kern, out_shape=(out, out, out), in_specs=[vm], out_specs=...]
    unnamed x7, local copies, waits for them, and re-layouts: 4.63 us -> 2.05 us
    pallas_call x1, Pallas kernels: 3.44 us -> 5.68 us  [trailing_update(): pl.pallas_call(kern, grid=(CC // step,), out_shape=jax.ShapeDtypeStruct((...]
  transfers between devices with their start and end apart: 3 -> 3, of which waited for: 2 -> 2; matrix products, arithmetic and copies ran while one was open for 1% -> 1% of each run, Pallas kernels for 39% -> 38%
where the time goes in v3:
time: 140 us; the launch traced here: 139 us
  Pallas kernels  59.1 us (42%)
  blocking collectives  38.8 us (28%)
  between operations  13.5 us (10%)
  waiting for transfers between devices  11 us (8%)
  starting transfers between devices  10.6 us (8%)
  local copies, waits for them, and re-layouts  4.91 us (4%)
    pallas_call x1, Pallas kernels, panel_solve(): pl.pallas_call(kern, out_shape=(out, out, jax.ShapeDtypeStruct((RR, PANEL...  43.8 us
    all_gather x1, blocking collectives, shards(): early = lax.all_gather(early, ('z', 'k'), axis=0, tiled=True)  27.6 us
    all_gather x1, blocking collectives, shards(): top = lax.all_gather(top, 'x', axis=0, tiled=True)  11.2 us
    all_to_all x1, starting transfers between devices, shards(): lax.all_to_all(block, ('y', 'x'), 0, 0, tiled=True).reshape(PR, thin)  10.5 us
    all_to_all x1, waiting for transfers between devices, shards(): lax.all_to_all(block, ('y', 'x'), 0, 0, tiled=True).reshape(PR, thin)  10.1 us
    pallas_call x1, Pallas kernels, first_blocks(): pl.pallas_call(kern, out_shape=(out, out, out), in_specs=[vm], out_specs=...  9.56 us
    pallas_call x1, Pallas kernels, trailing_update(): pl.pallas_call(kern, grid=(CC // step,), out_shape=jax.ShapeDtypeStruct((...  5.68 us
  transfers between devices with their start and end apart: 3, of which 2 were waited for; matrix products, arithmetic and copies ran while one was open for 1% of the time, Pallas kernels for 38%

profile of v3, /device:TPU:1, one launch (start us, length us, event | category | flops | bytes accessed | tf_op | source)
XLA Modules:
  0.0 139.3 jit_solution(8529004800808508133)
XLA Ops:
  6.5 0.0 slice-start
  6.5 0.8 slice.12
  7.3 0.1 broadcast_in_dim.7
  7.4 0.7 broadcast_in_dim.8
  8.1 10.5 %all-to-all-start = ((f32[32,16,128]{2,1,0:T(8,128)}), f32[32,16,128]{2,1,0:T(8,128)S(1)}, u32[]{:S(2)}, u32[]{:S(2)}) async-start(f32[32,16,128]{2,1,0:T(8,128)} %broadcast_in_dim.8), calls=%async_computation | async-start | bytes 524288 | tf_op jit(solution)/shard_map/all_to_all | solution.py:373
  18.6 0.0 all-gather.3.cloned.1.call-start
  18.7 0.9 slice.13
  19.6 0.1 copy.5
  19.7 10.1 %all-to-all-done = f32[32,16,128]{2,1,0:T(8,128)S(1)} async-done(((f32[32,16,128]{2,1,0:T(8,128)}), f32[32,16,128]{2,1,0:T(8,128)S(1)}, u32[]{:S(2)}, u32[]{:S(2)}) %all-to-all-start) | async-done | bytes 262176 | tf_op jit(solution)/shard_map/all_to_all | solution.py:373
  29.8 0.1 reshape.5
  30.0 0.2 copy.3
  30.2 0.8 pad_maximum_fusion
  30.9 0.0 all-gather.3.cloned.1.call-update
  31.0 0.0 all-gather.5.cloned.1.call-start
  31.0 27.6 %all_gather.13.a_ref = f32[512,256]{1,0:T(8,128)S(1)} all-gather(f32[32,256]{1,0:T(8,128)S(1)} %slice.16), channel_id=1, replica_groups=mesh['y'=8,'x'=4,'z'=8,'k'=2] {'z','k'}, dimensions={0}, use_global_device_ids=true | all-gather | bytes 557056 | tf_op jit(solution)/shard_map/all_gather | solution.py:378
  58.6 0.0 slice-done
  58.6 11.2 %all_gather.14 = f32[128,768]{1,0:T(8,128)} all-gather(f32[32,768]{1,0:T(8,128)S(1)} %slice-done), channel_id=1, replica_groups=mesh['y'=8,'x'=4,'z'=8,'k'=2] {'x'}, dimensions={0}, use_global_device_ids=true | all-gather | bytes 491520 | tf_op jit(solution)/shard_map/all_gather | solution.py:380
  69.8 0.0 all-gather.5.cloned.1.call-update
  69.9 0.6 pad_add_fusion.id_ref
  70.5 9.6 %first_blocks.1 = (f32[256,128]{1,0:T(8,128)S(1)}, f32[256,128]{1,0:T(8,128)S(1)}, f32[256,128]{1,0:T(8,128)S(1)}) custom-call(f32[512,256]{1,0:T(8,128)S(1)} %all_gather.13.a_ref), custom_call_target="tpu_custom_call" | custom-call | flops 15000000512 | bytes 2000000 | tf_op jit(solution)/shard_map/first_blocks/pallas_call | solution.py:153
  80.1 0.0 copy-start
  80.1 0.6 copy-done
  80.7 0.0 copy-start.1
  80.7 0.6 copy-done.1
  81.4 0.0 copy-start.2
  81.4 0.6 copy-done.2
  82.0 0.0 all-gather.3.cloned.1.call-done.pr_ref
  82.0 43.8 %panel_solve.1 = (bf16[384,1024]{1,0:T(8,128)(2,1)}, bf16[384,1024]{1,0:T(8,128)(2,1)}, f32[384,64]{1,0:T(8,128)}) custom-call(s32[2]{0:T(128)} %pad_add_fusion.id_ref, f32[1024,1408]{1,0:T(8,128)} %all-gather.3.cloned.1.call-done.pr_ref, f32[256,128]{1,0:T(8,128)} %copy-done, f32[256,128]{1,0:T(8,128)} %copy-done.1, f32[256,128]{1,0:T(8,128)} %copy-done.2), custom_call_target="tpu_custom_call" | custom-call | flops 30000001024 | bytes 8000000 | tf_op jit(solution)/shard_map/panel_solve/pallas_call | solution.py:311
  125.9 0.9 all-gather.5.cloned.1.call-done.ac
  126.8 5.7 %trailing_update.1 = f32[384,768]{1,0:T(8,128)} custom-call(bf16[384,1024]{1,0:T(8,128)(2,1)} %get-tuple-element.25.vth, bf16[384,1024]{1,0:T(8,128)(2,1)} %get-tuple-element.26.vtl, f32[384,64]{1,0:T(8,128)} %get-tuple-element.27.xc, f32[1024,768]{1,0:T(8,128)} %all-gather.5.cloned.1.call-done.ac, f32[384,768]{1,0:T(8,128)} %al.1), custom_call_target="tpu_custom_call" | custom-call | tf_op jit(solution)/shard_map/trailing_update/pallas_call | solution.py:354
  (1 shorter events, 0.0 us)
Async XLA Ops:
  6.5 52.1 %slice-start = ((f32[384,768]{1,0:T(8,128)}), f32[32,768]{1,0:T(8,128)S(1)}, s32[]{:S(2)}) async-start(f32[384,768]{1,0:T(8,128)} %al.1), calls=%async_computation.3 | async-start | bytes 196608 | tf_op jit(solution)/shard_map/slice | solution.py:379
  8.1 21.7 %all-to-all-start = ((f32[32,16,128]{2,1,0:T(8,128)}), f32[32,16,128]{2,1,0:T(8,128)S(1)}, u32[]{:S(2)}, u32[]{:S(2)}) async-start(f32[32,16,128]{2,1,0:T(8,128)} %broadcast_in_dim.8), calls=%async_computation | async-start | bytes 524288 | tf_op jit(solution)/shard_map/all_to_all | solution.py:373
  18.6 63.4 %all-gather.3.cloned.1.call-start = ((), (), s32[]{:S(2)}) async-start(), calls=%async_computation.1 | async-start | bytes 6127616 | tf_op jit(solution)/shard_map/all_gather | solution.py:377
  31.0 95.8 %all-gather.5.cloned.1.call-start = ((), (), s32[]{:S(2)}) async-start(), calls=%async_computation.2 | async-start | bytes 3538944 | tf_op jit(solution)/shard_map/all_gather | solution.py:383
  80.1 0.7 copy-start
  80.7 0.6 copy-start.1
  81.4 0.6 copy-start.2
Sparse Core Ops, SparseCore 0:
  31.1 49.6 all-gather.2
  82.9 43.8 all-gather.4

commit v4 on v3

--- a/solution.py
+++ b/solution.py
@@ -12,7 +12,7 @@
 PR = NB * PANELS
 B = 128
 KB = PR // B
-KA = 2
+KA = 3
 
 f32 = jnp.float32
 bf16 = jnp.bfloat16
@@ -62,8 +62,11 @@
             vals = [jnp.where(odd, vals[t + 1], vals[t]) for t in range(0, len(vals), 2)]
         return vals[0]
 
+    c = [lane_b(S[0], m) for m in range(8)]
     for s in range(16):
-        c = [lane_b(S[s], 8 * s + m) for m in range(8)]
+        if s < 15:
+            near = [lane_b(S[s + 1], 8 * s + m) for m in range(8)]
+            ahead = [lane_b(S[s + 1], 8 * s + 8 + m) for m in range(8)]
         a = {(t, m): sub_b(c[m], t) for m in range(8) for t in range(m, 8)}
         M = {}
         d = []
@@ -85,6 +88,9 @@
             for j in old:
                 a[max(i, j), min(i, j)] = scaled[j]
             a[i, i] = -p
+        if s < 15:
+            R = [tree([a[max(i, j), min(i, j)] * near[j] for j in range(8)]) for i in range(8)]
+            c = [ahead[m] + tree([near[i] * sub_b(R[i], m) for i in range(8)]) for m in range(8)]
         w = [column([a[max(t, m), min(t, m)] for t in range(8)]) for m in range(8)]
         YS = tree([w[m] * sub_b(S[s], m) for m in range(8)])
         YG = tree([w[m] * sub_b(G[s], m) for m in range(8)])
@@ -93,7 +99,7 @@
         ys = [sub_b(YS, m) for m in range(8)]
         yg = [sub_b(YG, m) for m in range(8)]
         for r in range(s + 1, 16):
-            b = [lane_b(S[r], 8 * s + m) for m in range(8)]
+            b = near if r == s + 1 else [lane_b(S[r], 8 * s + m) for m in range(8)]
             S[r] = S[r] + tree([b[m] * ys[m] for m in range(8)])
             G[r] = G[r] + tree([b[m] * yg[m] for m in range(8)])
         sq = [jnp.sqrt(d[i]) for i in range(8)]
@@ -120,7 +126,7 @@
 def first_blocks(a0):
     N = KA * B
 
-    def kern(a_ref, y0, g0, lbt0, E, D, LT, RHH, RLO):
+    def kern(a_ref, f0, E, D, LT, RHH, RLO):
         E[...] = a_ref[0:N, :]
         D[...] = E[0:B, 0:B]
         for k in range(KA):
@@ -134,10 +140,11 @@
                 u = u + dot(LT[j * B : (j + 1) * B, 0:B], RLO[:, k * B : N], NN)
                 E[j * B : (j + 1) * B, k * B : N] = E[j * B : (j + 1) * B, k * B : N] - u
 
-            factor128(D, y0.at[rows, :], g0.at[rows, :], lbt0.at[rows, :], fill)
+            y0, g0, lbt0 = (f0.at[n * N + k * B : n * N + (k + 1) * B, :] for n in range(3))
+            factor128(D, y0, g0, lbt0, fill)
             if k < KA - 1:
-                y = split(y0[rows, :])
-                g = split(g0[rows, :])
+                y = split(y0[...])
+                g = split(g0[...])
                 crit(E, D, y, g, k * B, (k + 1) * B)
                 h, l = split(dot3(y, split(E[rows, (k + 1) * B : N]), NN))
                 RHH[0:B, (k + 1) * B : N] = h
@@ -149,28 +156,27 @@
 
     vm = pl.BlockSpec(memory_space=pltpu.VMEM)
     V = pltpu.VMEM
-    out = jax.ShapeDtypeStruct((N, B), f32)
     return pl.pallas_call(
         kern,
-        out_shape=(out, out, out),
+        out_shape=jax.ShapeDtypeStruct((3 * N, B), f32),
         in_specs=[vm],
-        out_specs=(vm, vm, vm),
+        out_specs=vm,
         scratch_shapes=[V((N, N), f32), V((B, B), f32), V((N, 2 * B), bf16), V((2 * B, N), bf16), V((B, N), bf16)],
         compiler_params=pltpu.CompilerParams(vmem_limit_bytes=24 * 1024 * 1024),
-        cost_estimate=pl.CostEstimate(flops=15_000_000_000, bytes_accessed=2_000_000, transcendentals=0),
+        cost_estimate=pl.CostEstimate(flops=17_000_000_000, bytes_accessed=2_000_000, transcendentals=0),
         name="first_blocks",
     )(a0)
 
 
-def panel_solve(ids, gathered, y0, g0, lbt0):
+def panel_solve(ids, gathered, factors):
     W = gathered.shape[1]
     RR = W - PR
     n_col = PR // (PANELS * BS)
 
-    def kern(id_ref, pr_ref, y0, g0, lbt0, vth, vtl, xc, E, D, Y, G, LBT, YQ, GQ, LQ, LT, RHH, RLO, ZPH, ZPL, LRH, LRL, XT, sems):
+    def kern(id_ref, pr_ref, f0, vth, vtl, xc, E, D, Y, G, LBT, YQ, GQ, LQ, LT, RHH, RLO, ZPH, ZPL, LRH, LRL, XT, sems):
         copies = []
-        for c in range(n_col):
-            for p in range(PANELS):
+        for p in range(PANELS):
+            for c in range(n_col):
                 n = c * PANELS + p
                 copies.append(
                     pltpu.make_async_copy(
@@ -179,7 +185,7 @@
                 )
         for copy in copies:
             copy.start()
-        for copy in copies:
+        for copy in copies[: B // BS]:
             copy.wait()
         rid = id_ref[0]
         cid = id_ref[1]
@@ -259,10 +265,15 @@
             return [trail(j, c0, w) for j in range(first, KB) for c0, w in parts]
 
         for k in range(KA):
-            rows = slice(k * B, (k + 1) * B)
-            for q_ref, ref in ((YQ, y0), (GQ, g0), (LQ, lbt0)):
-                q_ref[0], q_ref[1] = split(ref[rows, :])
-            if k < KA - 1:
+            for n, ref in enumerate((YQ, GQ, LQ)):
+                ref[0], ref[1] = split(f0[(n * KA + k) * B : (n * KA + k + 1) * B, :])
+            if k == 0:
+                chunks = panel_chunks(k, k * B, k + 1)
+                drain(chunks[KB - 1 : KB + 3])
+                for copy in copies[B // BS :]:
+                    copy.wait()
+                drain(chunks[: KB - 1] + chunks[KB + 3 :] + trail_chunks(k + 1))
+            elif k < KA - 1:
                 drain(panel_chunks(k, k * B, k + 1) + trail_chunks(k + 1))
         crit(E, D, (YQ[0], YQ[1]), (GQ[0], GQ[1]), (KA - 1) * B, KA * B)
 
@@ -311,7 +322,7 @@
     return pl.pallas_call(
         kern,
         out_shape=(out, out, jax.ShapeDtypeStruct((RR, PANELS * BS), f32)),
-        in_specs=[pl.BlockSpec(memory_space=pltpu.SMEM), pl.BlockSpec(memory_space=pl.ANY), vm, vm, vm],
+        in_specs=[pl.BlockSpec(memory_space=pltpu.SMEM), pl.BlockSpec(memory_space=pl.ANY), vm],
         out_specs=(vm, vm, vm),
         scratch_shapes=[
             V((PR, W), f32),
@@ -333,9 +344,9 @@
             pltpu.SemaphoreType.DMA((PANELS * n_col,)),
         ],
         compiler_params=pltpu.CompilerParams(vmem_limit_bytes=58 * 1024 * 1024),
-        cost_estimate=pl.CostEstimate(flops=30_000_000_000, bytes_accessed=8_000_000, transcendentals=0),
+        cost_estimate=pl.CostEstimate(flops=46_000_000_000, bytes_accessed=8_000_000, transcendentals=0),
         name="panel_solve",
-    )(ids, gathered, y0, g0, lbt0)
+    )(ids, gathered, factors)
 
 
 def trailing_update(vth, vtl, xc, a_cols, local):
@@ -357,7 +368,7 @@
         out_shape=jax.ShapeDtypeStruct((RR, CC), f32),
         in_specs=[whole(vth), whole(vtl), whole(xc), part(PR), part(RR)],
         out_specs=part(RR),
-        compiler_params=pltpu.CompilerParams(vmem_limit_bytes=58 * 1024 * 1024),
+        compiler_params=pltpu.CompilerParams(vmem_limit_bytes=62 * 1024 * 1024),
         name="trailing_update",
     )(vth, vtl, xc, a_cols, local)
 
@@ -373,15 +384,13 @@
     own = lax.all_to_all(block, ("y", "x"), 0, 0, tiled=True).reshape(PR, thin).T
     mine = jnp.concatenate([own, matrix[:, :thin].T], axis=1)
     early = own[:BS, : KA * B]
-    mine, early = lax.optimization_barrier((mine, early))
+    mine, early, top = lax.optimization_barrier((mine, early, matrix[:BS]))
+    top = jnp.broadcast_to(top[None], (n_row,) + top.shape)
+    a_cols = lax.all_to_all(top, ("y", "x"), 0, 0, tiled=True).reshape(PR, top.shape[2])
     gathered = lax.all_gather(mine, ("z", "k"), axis=0, tiled=True)
     early = lax.all_gather(early, ("z", "k"), axis=0, tiled=True)
-    early, top = lax.optimization_barrier((early, matrix[:BS]))
-    top = lax.all_gather(top, "x", axis=0, tiled=True)
-    early, top = lax.optimization_barrier((early, top))
     factors = first_blocks(early)
-    a_cols = lax.all_gather(top, "y", axis=0, tiled=True)
-    vth, vtl, xc = panel_solve(ids, gathered, *factors)
+    vth, vtl, xc = panel_solve(ids, gathered, factors)
     return trailing_update(vth, vtl, xc, a_cols, matrix)
 
 

time: 140 us -> 133 us (0.950)
  blocking collectives: 38.8 us -> 30.5 us
  Pallas kernels: 59.1 us -> 53.4 us
  starting transfers between devices: 10.6 us -> 15.4 us
  waiting for transfers between devices: 11 us -> 12.6 us
    all_gather x1 -> x0, blocking collectives: 11.2 us -> none  [shards(): top = lax.all_gather(top, 'x', axis=0, tiled=True)]
    pallas_call x1, Pallas kernels: 43.8 us -> 36.4 us  [panel_solve(): pl.pallas_call(kern, out_shape=(out, out, jax.ShapeDtypeStruct((RR, PANEL...]
    all_to_all x0 -> x1, starting transfers between devices: none -> 4.88 us  [shards(): lax.all_to_all(top, ('y', 'x'), 0, 0, tiled=True).reshape(PR, top.shape[2])]
    all_gather x1, blocking collectives: 27.6 us -> 30.5 us  [shards(): early = lax.all_gather(early, ('z', 'k'), axis=0, tiled=True)]
    all_gather x1, waiting for transfers between devices: 0.01 us -> 2.45 us  [shards(): gathered = lax.all_gather(mine, ('z', 'k'), axis=0, tiled=True)]
    broadcast_in_dim x0 -> x1, local copies, waits for them, and re-layouts: none -> 1.98 us  [shards(): top = jnp.broadcast_to(top[None], (n_row,) + top.shape)]
    pallas_call x1, Pallas kernels: 9.56 us -> 11.3 us  [first_blocks(): pl.pallas_call(kern, out_shape=jax.ShapeDtypeStruct((3 * N, B), f32), in_...]
  transfers between devices with their start and end apart: 3 -> 3, of which waited for: 2 -> 2; matrix products, arithmetic and copies ran while one was open for 1% -> 3% of each run, Pallas kernels for 38% -> 36%
where the time goes in v4:
time: 133 us
  Pallas kernels  53.4 us (40%)
  blocking collectives  30.5 us (23%)
  starting transfers between devices  15.4 us (12%)
  between operations  13.5 us (10%)
  waiting for transfers between devices  12.6 us (9%)
  local copies, waits for them, and re-layouts  5.77 us (4%)
  other arithmetic  1.45 us (1%)
    pallas_call x1, Pallas kernels, panel_solve(): pl.pallas_call(kern, out_shape=(out, out, jax.ShapeDtypeStruct((RR, PANEL...  36.4 us
    all_gather x1, blocking collectives, shards(): early = lax.all_gather(early, ('z', 'k'), axis=0, tiled=True)  30.5 us
    pallas_call x1, Pallas kernels, first_blocks(): pl.pallas_call(kern, out_shape=jax.ShapeDtypeStruct((3 * N, B), f32), in_...  11.3 us
    all_to_all x1, starting transfers between devices, shards(): lax.all_to_all(block, ('y', 'x'), 0, 0, tiled=True).reshape(PR, thin)  10.5 us
    all_to_all x1, waiting for transfers between devices, shards(): lax.all_to_all(block, ('y', 'x'), 0, 0, tiled=True).reshape(PR, thin)  10.1 us
    pallas_call x1, Pallas kernels, trailing_update(): pl.pallas_call(kern, grid=(CC // step,), out_shape=jax.ShapeDtypeStruct((...  5.7 us
    all_to_all x1, starting transfers between devices, shards(): lax.all_to_all(top, ('y', 'x'), 0, 0, tiled=True).reshape(PR, top.shape[2])  4.88 us
  transfers between devices with their start and end apart: 3, of which 2 were waited for; matrix products, arithmetic and copies ran while one was open for 3% of the time, Pallas kernels for 36%

profile of v4, /device:TPU:1, one launch (start us, length us, event | category | flops | bytes accessed | tf_op | source)
XLA Modules:
  0.0 132.6 jit_solution(15935789060684693038)
XLA Ops:
  6.5 0.0 slice-start
  6.5 0.8 slice.12
  7.3 0.1 broadcast_in_dim.6
  7.4 0.7 broadcast_in_dim.14
  8.1 10.5 %all-to-all-start = ((f32[32,16,128]{2,1,0:T(8,128)}), f32[32,16,128]{2,1,0:T(8,128)S(1)}, u32[]{:S(2)}, u32[]{:S(2)}) async-start(f32[32,16,128]{2,1,0:T(8,128)} %broadcast_in_dim.14), calls=%async_computation | async-start | bytes 524288 | tf_op jit(solution)/shard_map/all_to_all | solution.py:384
  18.6 0.0 all-gather.2.cloned.1.call-start
  18.7 0.9 slice.13
  19.6 0.1 copy.5
  19.7 10.1 %all-to-all-done = f32[32,16,128]{2,1,0:T(8,128)S(1)} async-done(((f32[32,16,128]{2,1,0:T(8,128)}), f32[32,16,128]{2,1,0:T(8,128)S(1)}, u32[]{:S(2)}, u32[]{:S(2)}) %all-to-all-start) | async-done | bytes 262176 | tf_op jit(solution)/shard_map/all_to_all | solution.py:384
  29.8 0.1 reshape.9
  30.0 0.2 copy.3
  30.2 0.8 pad_maximum_fusion
  31.0 0.0 all-gather.2.cloned.1.call-update
  31.0 0.7 pad_add_fusion.id_ref
  31.7 0.0 slice-done
  31.7 2.0 %broadcast_in_dim.15 = f32[32,32,768]{2,1,0:T(8,128)} broadcast(f32[32,768]{1,0:T(8,128)S(1)} %slice-done), dimensions={1,2} | broadcast | bytes 3244032 | tf_op jit(solution)/shard_map/broadcast_in_dim | solution.py:388
  33.6 4.9 %all-to-all-start.1 = ((f32[32,32,768]{2,1,0:T(8,128)}), f32[32,32,768]{2,1,0:T(8,128)}, u32[]{:S(2)}, u32[]{:S(2)}) async-start(f32[32,32,768]{2,1,0:T(8,128)} %broadcast_in_dim.15), calls=%async_computation.1 | async-start | bytes 6291456 | tf_op jit(solution)/shard_map/all_to_all | solution.py:389
  38.5 30.5 %all_gather.7.a_ref = f32[512,384]{1,0:T(8,128)S(1)} all-gather(f32[32,384]{1,0:T(8,128)S(1)} %slice.16), channel_id=1, replica_groups=mesh['y'=8,'x'=4,'z'=8,'k'=2] {'z','k'}, dimensions={0}, use_global_device_ids=true | all-gather | bytes 835584 | tf_op jit(solution)/shard_map/all_gather | solution.py:391
  69.1 11.3 %first_blocks.1.f0 = f32[1152,128]{1,0:T(8,128)S(1)} custom-call(f32[512,384]{1,0:T(8,128)S(1)} %all_gather.7.a_ref), custom_call_target="tpu_custom_call" | custom-call | flops 16999999488 | bytes 2000000 | tf_op jit(solution)/shard_map/first_blocks/pallas_call | solution.py:159
  80.4 0.0 copy-start
  80.4 0.8 copy-done
  81.2 2.5 %all-gather.2.cloned.1.call-done.pr_ref = f32[1024,1408]{1,0:T(8,128)} async-done(((f32[64,1408]{1,0:T(8,128)}), f32[1024,1408]{1,0:T(8,128)}) %all-gather.2.cloned.1.call-update) | async-done | bytes 5767184 | tf_op jit(solution)/shard_map/all_gather | solution.py:390
  83.7 36.4 %panel_solve.1 = (bf16[384,1024]{1,0:T(8,128)(2,1)}, bf16[384,1024]{1,0:T(8,128)(2,1)}, f32[384,64]{1,0:T(8,128)}) custom-call(s32[2]{0:T(128)} %pad_add_fusion.id_ref, f32[1024,1408]{1,0:T(8,128)} %all-gather.2.cloned.1.call-done.pr_ref, f32[1152,128]{1,0:T(8,128)} %copy-done), custom_call_target="tpu_custom_call" | custom-call | flops 46000001024 | bytes 8000000 | tf_op jit(solution)/shard_map/panel_solve/pallas_call | solution.py:322
  120.0 0.0 all-to-all-done.1
  120.0 5.7 %trailing_update.1 = f32[384,768]{1,0:T(8,128)} custom-call(bf16[384,1024]{1,0:T(8,128)(2,1)} %get-tuple-element.13.vth, bf16[384,1024]{1,0:T(8,128)(2,1)} %get-tuple-element.14.vtl, f32[384,64]{1,0:T(8,128)} %get-tuple-element.15.xc, f32[1024,768]{1,0:T(8,128)} %bitcast.4.ac, f32[384,768]{1,0:T(8,128)} %al.1), custom_call_target="tpu_custom_call" | custom-call | tf_op jit(solution)/shard_map/trailing_update/pallas_call | solution.py:365
  (1 shorter events, 0.0 us)
Async XLA Ops:
  6.5 25.1 %slice-start = ((f32[384,768]{1,0:T(8,128)}), f32[32,768]{1,0:T(8,128)S(1)}, s32[]{:S(2)}) async-start(f32[384,768]{1,0:T(8,128)} %al.1), calls=%async_computation.3 | async-start | bytes 196608 | tf_op jit(solution)/shard_map/slice | solution.py:387
  8.1 21.7 %all-to-all-start = ((f32[32,16,128]{2,1,0:T(8,128)}), f32[32,16,128]{2,1,0:T(8,128)S(1)}, u32[]{:S(2)}, u32[]{:S(2)}) async-start(f32[32,16,128]{2,1,0:T(8,128)} %broadcast_in_dim.14), calls=%async_computation | async-start | bytes 524288 | tf_op jit(solution)/shard_map/all_to_all | solution.py:384
  18.6 65.0 %all-gather.2.cloned.1.call-start = ((), (), s32[]{:S(2)}) async-start(), calls=%async_computation.2 | async-start | bytes 6127616 | tf_op jit(solution)/shard_map/all_gather | solution.py:390
  33.6 86.4 %all-to-all-start.1 = ((f32[32,32,768]{2,1,0:T(8,128)}), f32[32,32,768]{2,1,0:T(8,128)}, u32[]{:S(2)}, u32[]{:S(2)}) async-start(f32[32,32,768]{2,1,0:T(8,128)} %broadcast_in_dim.15), calls=%async_computation.1 | async-start | bytes 6291456 | tf_op jit(solution)/shard_map/all_to_all | solution.py:389
  80.4 0.8 copy-start
Sparse Core Ops, SparseCore 0:
  31.1 52.5 all-gather.1

commit v5 on v4

--- a/solution.py
+++ b/solution.py
@@ -173,7 +173,7 @@
     RR = W - PR
     n_col = PR // (PANELS * BS)
 
-    def kern(id_ref, pr_ref, f0, vth, vtl, xc, E, D, Y, G, LBT, YQ, GQ, LQ, LT, RHH, RLO, ZPH, ZPL, LRH, LRL, XT, sems):
+    def kern(id_ref, pr_ref, f0, vth, vtl, xc, E, D, Y, G, LBT, YQ, GQ, LQ, LT, RHH, RLO, ZPH, ZPL, LRH, LRL, PV, XT, sems):
         copies = []
         for p in range(PANELS):
             for c in range(n_col):
@@ -277,35 +277,43 @@
                 drain(panel_chunks(k, k * B, k + 1) + trail_chunks(k + 1))
         crit(E, D, (YQ[0], YQ[1]), (GQ[0], GQ[1]), (KA - 1) * B, KA * B)
 
-        def body(k, carry):
-            q = k - 1
-            q0 = pl.multiple_of(q * B, B)
-            k0 = pl.multiple_of(k * B, B)
-            n0 = pl.multiple_of(jnp.minimum(k + 1, KB - 1) * B, B)
-            chunks = panel_chunks(q, q0, KA) + trail_chunks(KA)
+        def factor(chunks):
             n = len(chunks)
 
             def fill(s):
                 drain(chunks[n * s // 16 : n * (s + 1) // 16])
 
             factor128(D, Y, G, LBT, fill)
-            y = split(Y[...])
-            g = split(G[...])
-            lb = split(LBT[...])
-            for i in range(2):
-                YQ[i] = y[i]
-                GQ[i] = g[i]
-                LQ[i] = lb[i]
-            crit(E, D, y, g, k0, n0)
+            for q_ref, ref in ((YQ, Y), (GQ, G), (LQ, LBT)):
+                q_ref[0], q_ref[1] = split(ref[...])
+
+        def body(k, carry):
+            q0 = pl.multiple_of((k - 1) * B, B)
+            k0 = pl.multiple_of(k * B, B)
+            n0 = pl.multiple_of((k + 1) * B, B)
+            factor(panel_chunks(k - 1, q0, KA) + trail_chunks(KA))
+            crit(E, D, split(Y[...]), split(G[...]), k0, n0)
             return carry
 
-        lax.fori_loop(KA, KB, body, 0)
-        drain(panel_chunks(KB - 1, (KB - 1) * B, KB))
-        for c0 in range(0, PR, 256):
-            for ref in (ZPH, ZPL):
-                ref[c0 : c0 + B, c0 + B : c0 + 2 * B] = jnp.zeros((B, B), bf16)
-            z = (ZPH[c0:PR, c0 : c0 + 256], ZPL[c0:PR, c0 : c0 + 256])
-            h, l = split(dot3((LRH[:, c0:PR], LRL[:, c0:PR]), z, NN))
+        def inverse(rows, c0):
+            z = (ZPH[rows, c0 : c0 + 256], ZPL[rows, c0 : c0 + 256])
+            return dot3((LRH[:, rows], LRL[:, rows]), z, NN)
+
+        def partial(c0):
+            def f():
+                for ref in (ZPH, ZPL):
+                    ref[c0 : c0 + B, c0 + B : c0 + 2 * B] = jnp.zeros((B, B), bf16)
+                PV[:, c0 : c0 + 256] = inverse(slice(c0, last), c0)
+
+            return f
+
+        lax.fori_loop(KA, KB - 1, body, 0)
+        last = (KB - 1) * B
+        steps = range(0, PR, 256)
+        factor(panel_chunks(KB - 2, last - B, KB - 1) + trail_chunks(KB - 1) + [partial(c0) for c0 in steps])
+        drain(panel_chunks(KB - 1, last, KB))
+        for c0 in steps:
+            h, l = split(PV[:, c0 : c0 + 256] + inverse(slice(last, PR), c0))
             vth[:, c0 : c0 + 256] = h
             vtl[:, c0 : c0 + 256] = l
         for p in range(PANELS):
@@ -340,6 +348,7 @@
             V((PR, PR), bf16),
             V((RR, PR), bf16),
             V((RR, PR), bf16),
+            V((RR, PR), f32),
             V((PR, RR), f32),
             pltpu.SemaphoreType.DMA((PANELS * n_col,)),
         ],

time: 133 us -> 132 us (level)
  no operation moved by 1% of the time
where the time goes in v5:
time: 132 us
  Pallas kernels  52.8 us (40%)
  blocking collectives  30.5 us (23%)
  starting transfers between devices  15.4 us (12%)
  between operations  13.5 us (10%)
  waiting for transfers between devices  12.6 us (10%)
  local copies, waits for them, and re-layouts  5.77 us (4%)
  other arithmetic  1.45 us (1%)
    pallas_call x1, Pallas kernels, panel_solve(): pl.pallas_call(kern, out_shape=(out, out, jax.ShapeDtypeStruct((RR, PANEL...  35.8 us
    all_gather x1, blocking collectives, shards(): early = lax.all_gather(early, ('z', 'k'), axis=0, tiled=True)  30.5 us
    pallas_call x1, Pallas kernels, first_blocks(): pl.pallas_call(kern, out_shape=jax.ShapeDtypeStruct((3 * N, B), f32), in_...  11.3 us
    all_to_all x1, starting transfers between devices, shards(): lax.all_to_all(block, ('y', 'x'), 0, 0, tiled=True).reshape(PR, thin)  10.5 us
    all_to_all x1, waiting for transfers between devices, shards(): lax.all_to_all(block, ('y', 'x'), 0, 0, tiled=True).reshape(PR, thin)  10.1 us
    pallas_call x1, Pallas kernels, trailing_update(): pl.pallas_call(kern, grid=(CC // step,), out_shape=jax.ShapeDtypeStruct((...  5.7 us
    all_to_all x1, starting transfers between devices, shards(): lax.all_to_all(top, ('y', 'x'), 0, 0, tiled=True).reshape(PR, top.shape[2])  4.88 us
  transfers between devices with their start and end apart: 3, of which 2 were waited for; matrix products, arithmetic and copies ran while one was open for 3% of the time, Pallas kernels for 36%

profile of v5, /device:TPU:1, one launch (start us, length us, event | category | flops | bytes accessed | tf_op | source)
XLA Modules:
  0.0 132.0 jit_solution(538770783301440303)
XLA Ops:
  6.5 0.0 slice-start
  6.5 0.8 slice.12
  7.3 0.1 broadcast_in_dim.6
  7.4 0.7 broadcast_in_dim.14
  8.1 10.5 %all-to-all-start = ((f32[32,16,128]{2,1,0:T(8,128)}), f32[32,16,128]{2,1,0:T(8,128)S(1)}, u32[]{:S(2)}, u32[]{:S(2)}) async-start(f32[32,16,128]{2,1,0:T(8,128)} %broadcast_in_dim.14), calls=%async_computation | async-start | bytes 524288 | tf_op jit(solution)/shard_map/all_to_all | solution.py:393
  18.6 0.0 all-gather.2.cloned.1.call-start
  18.7 0.9 slice.13
  19.6 0.1 copy.5
  19.7 10.1 %all-to-all-done = f32[32,16,128]{2,1,0:T(8,128)S(1)} async-done(((f32[32,16,128]{2,1,0:T(8,128)}), f32[32,16,128]{2,1,0:T(8,128)S(1)}, u32[]{:S(2)}, u32[]{:S(2)}) %all-to-all-start) | async-done | bytes 262176 | tf_op jit(solution)/shard_map/all_to_all | solution.py:393
  29.8 0.1 reshape.9
  30.0 0.2 copy.3
  30.2 0.8 pad_maximum_fusion
  31.0 0.0 all-gather.2.cloned.1.call-update
  31.0 0.7 pad_add_fusion.id_ref
  31.7 0.0 slice-done
  31.7 2.0 %broadcast_in_dim.15 = f32[32,32,768]{2,1,0:T(8,128)} broadcast(f32[32,768]{1,0:T(8,128)S(1)} %slice-done), dimensions={1,2} | broadcast | bytes 3244032 | tf_op jit(solution)/shard_map/broadcast_in_dim | solution.py:397
  33.6 4.9 %all-to-all-start.1 = ((f32[32,32,768]{2,1,0:T(8,128)}), f32[32,32,768]{2,1,0:T(8,128)}, u32[]{:S(2)}, u32[]{:S(2)}) async-start(f32[32,32,768]{2,1,0:T(8,128)} %broadcast_in_dim.15), calls=%async_computation.1 | async-start | bytes 6291456 | tf_op jit(solution)/shard_map/all_to_all | solution.py:398
  38.5 30.5 %all_gather.7.a_ref = f32[512,384]{1,0:T(8,128)S(1)} all-gather(f32[32,384]{1,0:T(8,128)S(1)} %slice.16), channel_id=1, replica_groups=mesh['y'=8,'x'=4,'z'=8,'k'=2] {'z','k'}, dimensions={0}, use_global_device_ids=true | all-gather | bytes 835584 | tf_op jit(solution)/shard_map/all_gather | solution.py:400
  69.1 11.3 %first_blocks.1.f0 = f32[1152,128]{1,0:T(8,128)S(1)} custom-call(f32[512,384]{1,0:T(8,128)S(1)} %all_gather.7.a_ref), custom_call_target="tpu_custom_call" | custom-call | flops 16999999488 | bytes 2000000 | tf_op jit(solution)/shard_map/first_blocks/pallas_call | solution.py:159
  80.4 0.0 copy-start
  80.4 0.8 copy-done
  81.2 2.5 %all-gather.2.cloned.1.call-done.pr_ref = f32[1024,1408]{1,0:T(8,128)} async-done(((f32[64,1408]{1,0:T(8,128)}), f32[1024,1408]{1,0:T(8,128)}) %all-gather.2.cloned.1.call-update) | async-done | bytes 5767184 | tf_op jit(solution)/shard_map/all_gather | solution.py:399
  83.7 35.8 %panel_solve.1 = (bf16[384,1024]{1,0:T(8,128)(2,1)}, bf16[384,1024]{1,0:T(8,128)(2,1)}, f32[384,64]{1,0:T(8,128)}) custom-call(s32[2]{0:T(128)} %pad_add_fusion.id_ref, f32[1024,1408]{1,0:T(8,128)} %all-gather.2.cloned.1.call-done.pr_ref, f32[1152,128]{1,0:T(8,128)} %copy-done), custom_call_target="tpu_custom_call" | custom-call | flops 46000001024 | bytes 8000000 | tf_op jit(solution)/shard_map/panel_solve/pallas_call | solution.py:330
  119.4 0.0 all-to-all-done.1
  119.4 5.7 %trailing_update.1 = f32[384,768]{1,0:T(8,128)} custom-call(bf16[384,1024]{1,0:T(8,128)(2,1)} %get-tuple-element.13.vth, bf16[384,1024]{1,0:T(8,128)(2,1)} %get-tuple-element.14.vtl, f32[384,64]{1,0:T(8,128)} %get-tuple-element.15.xc, f32[1024,768]{1,0:T(8,128)} %bitcast.4.ac, f32[384,768]{1,0:T(8,128)} %al.1), custom_call_target="tpu_custom_call" | custom-call | tf_op jit(solution)/shard_map/trailing_update/pallas_call | solution.py:374
  (1 shorter events, 0.0 us)
Async XLA Ops:
  6.5 25.1 %slice-start = ((f32[384,768]{1,0:T(8,128)}), f32[32,768]{1,0:T(8,128)S(1)}, s32[]{:S(2)}) async-start(f32[384,768]{1,0:T(8,128)} %al.1), calls=%async_computation.3 | async-start | bytes 196608 | tf_op jit(solution)/shard_map/slice | solution.py:396
  8.1 21.7 %all-to-all-start = ((f32[32,16,128]{2,1,0:T(8,128)}), f32[32,16,128]{2,1,0:T(8,128)S(1)}, u32[]{:S(2)}, u32[]{:S(2)}) async-start(f32[32,16,128]{2,1,0:T(8,128)} %broadcast_in_dim.14), calls=%async_computation | async-start | bytes 524288 | tf_op jit(solution)/shard_map/all_to_all | solution.py:393
  18.6 65.0 %all-gather.2.cloned.1.call-start = ((), (), s32[]{:S(2)}) async-start(), calls=%async_computation.2 | async-start | bytes 6127616 | tf_op jit(solution)/shard_map/all_gather | solution.py:399
  33.6 85.8 %all-to-all-start.1 = ((f32[32,32,768]{2,1,0:T(8,128)}), f32[32,32,768]{2,1,0:T(8,128)}, u32[]{:S(2)}, u32[]{:S(2)}) async-start(f32[32,32,768]{2,1,0:T(8,128)} %broadcast_in_dim.15), calls=%async_computation.1 | async-start | bytes 6291456 | tf_op jit(solution)/shard_map/all_to_all | solution.py:398
  80.4 0.8 copy-start
Sparse Core Ops, SparseCore 0:
  31.1 52.5 all-gather.1
